TPU v7x, 32 devices: a whole 2x2x4 slice. The times are simulated.
32 devices in a mesh: dp: 2 (over y), expert: 16 (over z, x, core).
Axes of the slice: x: 2, y: 2, z: 4, core: 2. Of those that a mesh axis runs over, the one named last changes fastest.
Arguments:
- tokens: bfloat16 [2048, 4096], P('expert', 'dp'), may hold values from -6 to 6
- expert_ids: int32 [2048, 8], P('expert'), may hold values from 0 to 31, all different within a row; in each aligned block of 128 rows (0 to 127, 128 to 255, ...) at most 48 rows name the same one
- route_weights: float32 [2048, 8], P('expert'), may hold values from 0.1 to 0.4
- gate_up_weight: bfloat16 [32, 4096, 1536], P('expert', 'dp'), may hold values from -0.09375 to 0.09375
- down_weight: bfloat16 [32, 768, 4096], P('expert', None, 'dp'), may hold values from -0.21875 to 0.21875
- out_grad: bfloat16 [2048, 4096], P('expert', 'dp'), may hold values from -6 to 6
Outputs:
- layer_out: bfloat16 [2048, 4096], P('expert', 'dp')
- token_grad: bfloat16 [2048, 4096], P('expert', 'dp')
- route_grad: float32 [2048, 8], P('expert')
- gate_up_grad: bfloat16 [32, 4096, 1536], P('expert', 'dp')
- down_grad: bfloat16 [32, 768, 4096], P('expert', None, 'dp')
Inputs may be any that keep to these rules, and one draw needn't show every extreme that they name: `expert_ids`: each row names 8 different experts. Among the 128 rows of one group no expert is named more than 48 times, and in every draw some group names some expert exactly 48 times.
All inputs are finite; a program needn't handle non-finite values.
Results may differ from a plain program's by a relative error of at most 0.029.
Values may be sent and summed in bfloat16 or wider, within the bound.
A program may use at most 128 MiB of HBM per device.

v0:
```python
import jax
import jax.numpy as jnp
from jax import lax
from jax.sharding import PartitionSpec as P


def local(tokens, expert_ids, route_weights, gate_up_weight, down_weight, out_grad):
    tok_count, piece_width = tokens.shape
    top_count = expert_ids.shape[1]
    group_count = lax.axis_size("expert")
    local_count = gate_up_weight.shape[0]
    hidden_units = down_weight.shape[1]
    expert_total = local_count * group_count
    capacity = 3 * tok_count * top_count // (2 * expert_total)
    slot_count = expert_total * capacity
    rows_all = group_count * capacity
    route_count = tok_count * top_count
    block_shape = (local_count, group_count, capacity, piece_width)
    route_ids = expert_ids.reshape(-1)
    onehot = (route_ids[:, None] == jnp.arange(expert_total, dtype=jnp.int32)[None, :]).astype(
        jnp.int32
    )
    slot_rank = jnp.sum(onehot * (jnp.cumsum(onehot, axis=0) - 1), axis=1)
    slot_index = (
        route_ids % local_count * rows_all + route_ids // local_count * capacity + slot_rank
    )
    slot_route = (
        jnp.full((slot_count,), route_count, jnp.int32)
        .at[slot_index]
        .set(jnp.arange(route_count, dtype=jnp.int32))
    )
    source_tok = slot_route // top_count
    weight_flat = route_weights.reshape(-1)
    weight_padded = jnp.concatenate([weight_flat, jnp.zeros((1,), jnp.float32)], axis=0)
    tokens_padded = jnp.concatenate([tokens, jnp.zeros((1, piece_width), tokens.dtype)], axis=0)
    grad_padded = jnp.concatenate([out_grad, jnp.zeros((1, piece_width), out_grad.dtype)], axis=0)
    outbound = tokens_padded[source_tok]
    grad_outbound = (
        weight_padded[slot_route][:, None] * grad_padded[source_tok].astype(jnp.float32)
    ).astype(jnp.bfloat16)
    arrived, grad_arrived = (
        lax.all_to_all(
            outbound.reshape(block_shape), "expert", split_axis=1, concat_axis=1, tiled=True
        ),
        lax.all_to_all(
            grad_outbound.reshape(block_shape), "expert", split_axis=1, concat_axis=1, tiled=True
        ),
    )
    arrived = arrived.reshape(local_count, rows_all, piece_width)
    grad_arrived = grad_arrived.reshape(local_count, rows_all, piece_width)
    rows = arrived
    preact = lax.psum_scatter(
        jnp.einsum("lrk,lkf->rlf", rows, gate_up_weight, preferred_element_type=jnp.float32).astype(
            jnp.bfloat16
        ),
        "dp",
        scatter_dimension=0,
        tiled=True,
    ).astype(jnp.float32)
    gate_pre = preact[..., :hidden_units]
    up_pre = preact[..., hidden_units:]
    sigmoid_gate = jax.nn.sigmoid(gate_pre)
    activation = gate_pre * sigmoid_gate
    hidden_mine = (activation * up_pre).astype(jnp.bfloat16)
    hidden_all = lax.all_gather(hidden_mine, "dp", axis=0, tiled=True)
    out_slice = jnp.einsum(
        "rlf,lfk->lrk", hidden_all, down_weight, preferred_element_type=jnp.float32
    ).astype(jnp.bfloat16)
    grad_routes = jnp.repeat(out_grad, top_count, axis=0).astype(jnp.float32)
    returned = lax.all_to_all(
        out_slice.reshape(block_shape), "expert", split_axis=1, concat_axis=1, tiled=True
    )
    y_routes = returned.reshape(slot_count, piece_width)[slot_index].astype(jnp.float32)
    layer_out = (
        (weight_flat[:, None] * y_routes)
        .reshape(tok_count, top_count, piece_width)
        .sum(axis=1)
        .astype(jnp.bfloat16)
    )
    partial_dot = jnp.sum(grad_routes * y_routes, axis=1).reshape(tok_count, top_count)
    route_grad = lax.psum(partial_dot, "dp")
    layer_out, route_grad = (layer_out, route_grad)
    rows = grad_arrived
    hidden_grad = lax.psum_scatter(
        jnp.einsum("lrk,lfk->rlf", rows, down_weight, preferred_element_type=jnp.float32).astype(
            jnp.bfloat16
        ),
        "dp",
        scatter_dimension=0,
        tiled=True,
    ).astype(jnp.float32)
    gate_grad = hidden_grad * up_pre * sigmoid_gate * (1.0 + gate_pre * (1.0 - sigmoid_gate))
    up_grad = hidden_grad * activation
    preact_grad = jnp.concatenate([gate_grad, up_grad], axis=2).astype(jnp.bfloat16)
    preact_grad_all = lax.all_gather(preact_grad, "dp", axis=0, tiled=True)
    x_grad_slice = jnp.einsum(
        "rlf,lkf->lrk", preact_grad_all, gate_up_weight, preferred_element_type=jnp.float32
    ).astype(jnp.bfloat16)
    gate_up_grad = jnp.einsum(
        "lrk,rlf->lkf", arrived, preact_grad_all, preferred_element_type=jnp.float32
    ).astype(jnp.bfloat16)
    down_grad = jnp.einsum(
        "rlf,lrk->lfk", hidden_all, grad_arrived, preferred_element_type=jnp.float32
    ).astype(jnp.bfloat16)
    grad_back = lax.all_to_all(
        x_grad_slice.reshape(block_shape), "expert", split_axis=1, concat_axis=1, tiled=True
    )
    grad_per_route = grad_back.reshape(slot_count, piece_width)[slot_index].astype(jnp.float32)
    token_grad = (
        grad_per_route.reshape(tok_count, top_count, piece_width).sum(axis=1).astype(jnp.bfloat16)
    )
    return (layer_out, token_grad, route_grad, gate_up_grad, down_grad)


def solution(mesh):
    placed = (
        P("expert", "dp"),
        P("expert", None),
        P("expert", None),
        P("expert", "dp", None),
        P("expert", None, "dp"),
        P("expert", "dp"),
    )
    return jax.shard_map(
        local,
        mesh=mesh,
        in_specs=placed,
        out_specs=(
            P("expert", "dp"),
            P("expert", "dp"),
            P("expert", None),
            P("expert", "dp", None),
            P("expert", None, "dp"),
        ),
        check_vma=False,
    )
```

profile of v0, /device:TPU:11, one launch (start us, length us, event | category | flops | bytes accessed | tf_op | source)
XLA Modules:
  0.0 743.7 jit_solution(11894425971731801471)
XLA Ops:
  7.2 0.8 copy.43
  8.3 9.0 %reduce-window.6 = s32[32,8,128]{2,1,0:T(8,128)S(1)} reduce-window(s32[32,8,128]{2,1,0:T(8,128)S(1)} %fusion.11, s32[]{:T(128)} %constant.55.clone.1), window={size=1x1x128 pad=0_0x0_0x127_0}, to_apply=%region_0.0 | reduce-window | flops 4161536 | bytes 262148 | tf_op jit(solution)/shard_map/reduce-window
  17.4 0.1 copy.46
  17.8 4.3 scatter_custom_fusion
  22.2 1.1 concatenate.13
  23.3 7.0 gather_fusion
  30.2 6.5 copy.48
  36.8 6.7 all-to-all-start
  43.6 0.6 copy-done.3
  44.3 8.4 %gather_fusion.2 = f32[1536]{0:T(1024)S(1)} fusion(f32[1025]{0:T(1024)S(1)} %pad_maximum_fusion.1, s32[2048]{0:T(1024)S(1)} %get-tuple-element.25), kind=kCustom, calls=%fused_computation.2 | custom fusion | bytes 18432 | tf_op jit(solution)/shard_map/gather | solution.py:39
  52.9 7.0 gather_fusion.3
  59.9 6.6 fusion
  66.4 114.5 %all-to-all-done = bf16[2,16,48,2048]{3,2,0,1:T(8,128)(2,1)} async-done(((bf16[2,16,48,2048]{3,2,0,1:T(8,128)(2,1)}), bf16[2,16,48,2048]{3,2,0,1:T(8,128)(2,1)}, u32[]{:S(2)}, u32[]{:S(2)}) %all-to-all-start) | async-done | bytes 6291488 | tf_op jit(solution)/shard_map/all_to_all | solution.py:42
  180.9 4.9 all-to-all-start.2
  185.8 3.4 copy.49
  189.2 2.7 copy-done
  191.9 14.3 %convert_bitcast_fusion.1 = bf16[768,2,1536]{2,0,1:T(8,128)(2,1)} fusion(bf16[2,768,2048]{2,1,0:T(8,128)(2,1)S(1)} %bitcast.56, bf16[2,2048,1536]{2,1,0:T(8,128)(2,1)} %param.9), kind=kOutput, calls=%fused_computation.14 | convolution fusion | flops 9666035712 | bytes 23592960 | tf_op jit(solution)/shard_map/lrk,lkf->rlf/dot_general | solution.py:53
  206.2 0.2 reduce-scatter.5.cloned.1.call-start
  206.4 116.8 %all-to-all-done.2 = bf16[2,16,48,2048]{3,2,0,1:T(8,128)(2,1)} async-done(((bf16[2,16,48,2048]{3,2,0,1:T(8,128)(2,1)}), bf16[2,16,48,2048]{3,2,0,1:T(8,128)(2,1)}, u32[]{:S(2)}, u32[]{:S(2)}) %all-to-all-start.2) | async-done | bytes 6291488 | tf_op jit(solution)/shard_map/all_to_all | solution.py:45
  323.2 3.4 copy.55
  326.6 2.7 copy-done.1
  329.3 9.2 %convert_bitcast_fusion.2 = bf16[768,2,768]{2,0,1:T(8,128)(2,1)} fusion(bf16[2,768,2048]{2,1,0:T(8,128)(2,1)S(1)} %bitcast.60, bf16[2,768,2048]{2,1,0:T(8,128)(2,1)} %param.10), kind=kOutput, calls=%fused_computation.26 | convolution fusion | flops 4833017856 | bytes 14942208 | tf_op jit(solution)/shard_map/lrk,lfk->rlf/dot_general | solution.py:85
  338.5 4.5 convert_element_type.77
  343.0 29.8 %reduce-scatter.5.cloned.1.call-done = bf16[384,2,768]{2,0,1:T(8,128)(2,1)} async-done(((bf16[768,2,768]{2,0,1:T(8,128)(2,1)}), bf16[384,2,768]{2,0,1:T(8,128)(2,1)}) %reduce-scatter.5.cloned.1.call-update) | async-done | bytes 1179664 | tf_op jit(solution)/shard_map/reduce_scatter | solution.py:84
  372.8 5.2 fusion.6
  378.0 36.2 %all-gather.3.cloned.1.call-done = bf16[768,2,768]{2,0,1:T(8,128)(2,1)} async-done(((bf16[384,2,768]{2,0,1:T(8,128)(2,1)}), bf16[768,2,768]{2,0,1:T(8,128)(2,1)}) %all-gather.3.cloned.1.call-update) | async-done | bytes 2359312 | tf_op jit(solution)/shard_map/all_gather | solution.py:65
  414.2 7.8 %convolution_convert_fusion.3 = bf16[2,768,2048]{2,1,0:T(8,128)(2,1)S(1)} fusion(bf16[768,2,768]{2,0,1:T(8,128)(2,1)} %all-gather.3.cloned.1.call-done, bf16[2,768,2048]{2,1,0:T(8,128)(2,1)} %param.10), kind=kOutput, calls=%fused_computation.17 | convolution fusion | flops 4834983936 | bytes 14942208 | tf_op jit(solution)/shard_map/rlf,lfk->lrk/dot_general | solution.py:66
  422.1 3.3 copy.50
  425.4 6.4 all-to-all-start.1
  431.8 1.6 pad_maximum_fusion
  433.5 62.7 %all-gather.5.cloned.1.call-done = bf16[768,2,1536]{2,0,1:T(8,128)(2,1)} async-done(((bf16[384,2,1536]{2,0,1:T(8,128)(2,1)}), bf16[768,2,1536]{2,0,1:T(8,128)(2,1)}) %all-gather.5.cloned.1.call-update) | async-done | bytes 4718608 | tf_op jit(solution)/shard_map/all_gather | solution.py:95
  496.2 14.4 %convolution_convert_fusion.2 = bf16[2,768,2048]{2,1,0:T(8,128)(2,1)S(1)} fusion(bf16[768,2,1536]{2,0,1:T(8,128)(2,1)} %all-gather.5.cloned.1.call-done, bf16[2,2048,1536]{2,1,0:T(8,128)(2,1)} %param.9), kind=kOutput, calls=%fused_computation.16 | convolution fusion | flops 9666822144 | bytes 23592960 | tf_op jit(solution)/shard_map/rlf,lkf->lrk/dot_general | solution.py:96
  510.6 3.2 copy.56
  513.7 55.4 %all-to-all-done.1 = bf16[2,16,48,2048]{3,2,0,1:T(8,128)(2,1)} async-done(((bf16[2,16,48,2048]{3,2,0,1:T(8,128)(2,1)}), bf16[2,16,48,2048]{3,2,0,1:T(8,128)(2,1)}, u32[]{:S(2)}, u32[]{:S(2)}) %all-to-all-start.1) | async-done | bytes 6291488 | tf_op jit(solution)/shard_map/all_to_all | solution.py:70
  569.2 5.4 all-to-all-start.3
  574.6 1.3 convert_element_type.90
  575.9 9.8 %convolution_convert_fusion.1 = bf16[2,768,2048]{2,1,0:T(8,128)(2,1)} fusion(bf16[768,2,768]{2,0,1:T(8,128)(2,1)} %all-gather.3.cloned.1.call-done, bf16[2,768,2048]{2,1,0:T(8,128)(2,1)} %bitcast.61), kind=kOutput, calls=%fused_computation.15 | convolution fusion | flops 4834983936 | bytes 14942208 | tf_op jit(solution)/shard_map/rlf,lrk->lfk/dot_general | solution.py:102
  585.7 12.4 %convolution_convert_fusion = bf16[2,2048,1536]{2,1,0:T(8,128)(2,1)} fusion(bf16[2,768,2048]{2,1,0:T(8,128)(2,1)S(1)} %bitcast.59, bf16[768,2,1536]{2,0,1:T(8,128)(2,1)S(1)} %bitcast.70), kind=kOutput, calls=%fused_computation.8 | convolution fusion | flops 9669967872 | bytes 23592960 | tf_op jit(solution)/shard_map/lrk,rlf->lkf/dot_general | solution.py:99
  598.1 6.6 copy.51
  604.7 12.4 %gather_fusion.1 = bf16[1024,2048]{1,0:T(8,128)(2,1)} fusion(bf16[1536,2048]{1,0:T(8,128)(2,1)} %bitcast.53, s32[1024]{0:T(1024)S(1)} %broadcast_clamp_fusion), kind=kCustom, calls=%fused_computation.1 | custom fusion | bytes 8392704 | tf_op jit(solution)/shard_map/gather | solution.py:73
  617.1 3.1 fusion.3
  620.3 6.1 psum.7
  626.5 0.7 copy.60
  627.1 7.3 fusion.2
  634.4 77.4 %all-to-all-done.3 = bf16[2,16,48,2048]{3,2,0,1:T(8,128)(2,1)} async-done(((bf16[2,16,48,2048]{3,2,0,1:T(8,128)(2,1)}), bf16[2,16,48,2048]{3,2,0,1:T(8,128)(2,1)}, u32[]{:S(2)}, u32[]{:S(2)}) %all-to-all-start.3) | async-done | bytes 6291488 | tf_op jit(solution)/shard_map/all_to_all | solution.py:105
  711.8 6.6 copy.57
  718.4 12.4 %gather_fusion.4 = bf16[1024,2048]{1,0:T(8,128)(2,1)} fusion(bf16[1536,2048]{1,0:T(8,128)(2,1)} %bitcast.52, s32[1024]{0:T(1024)S(1)} %broadcast_clamp_fusion), kind=kCustom, calls=%fused_computation.4 | custom fusion | bytes 8392704 | tf_op jit(solution)/shard_map/gather | solution.py:108
  730.8 5.9 bitcast_reduce_fusion
  (49 shorter events, 1.4 us)
Async XLA Ops:
  36.8 6.7 copy-start.5
  36.8 144.1 %all-to-all-start = ((bf16[2,16,48,2048]{3,2,0,1:T(8,128)(2,1)}), bf16[2,16,48,2048]{3,2,0,1:T(8,128)(2,1)}, u32[]{:S(2)}, u32[]{:S(2)}) async-start(bf16[2,16,48,2048]{3,2,0,1:T(8,128)(2,1)} %copy.48), calls=%async_computation | async-start | bytes 12582912 | tf_op jit(solution)/shard_map/all_to_all | solution.py:42
  43.5 9.3 %copy-start.2 = (bf16[128,2048]{1,0:T(8,128)(2,1)S(1)}, bf16[128,2048]{1,0:T(8,128)(2,1)}, u32[]{:S(2)}) copy-start(bf16[128,2048]{1,0:T(8,128)(2,1)} %param.11) | copy-start | bytes 1572868
  43.6 0.6 copy-start.3
  180.9 142.3 %all-to-all-start.2 = ((bf16[2,16,48,2048]{3,2,0,1:T(8,128)(2,1)}), bf16[2,16,48,2048]{3,2,0,1:T(8,128)(2,1)}, u32[]{:S(2)}, u32[]{:S(2)}) async-start(bf16[2,16,48,2048]{3,2,0,1:T(8,128)(2,1)} %fusion), calls=%async_computation.3 | async-start | bytes 12582912 | tf_op jit(solution)/shard_map/all_to_all | solution.py:45
  185.8 152.7 %reduce-scatter.3.cloned.1.call-start = ((), (), s32[]{:S(2)}) async-start(), calls=%async_computation.6 | async-start | bytes 7077888 | tf_op jit(solution)/shard_map/reduce_scatter | solution.py:52
  189.2 2.7 copy-start
  206.2 166.7 %reduce-scatter.5.cloned.1.call-start = ((), (), s32[]{:S(2)}) async-start(), calls=%async_computation.8 | async-start | bytes 3538944 | tf_op jit(solution)/shard_map/reduce_scatter | solution.py:84
  326.6 2.7 copy-start.1
  338.5 75.8 %all-gather.3.cloned.1.call-start = ((), (), s32[]{:S(2)}) async-start(), calls=%async_computation.7 | async-start | bytes 3538944 | tf_op jit(solution)/shard_map/all_gather | solution.py:65
  425.4 143.8 %all-to-all-start.1 = ((bf16[2,16,48,2048]{3,2,0,1:T(8,128)(2,1)}), bf16[2,16,48,2048]{3,2,0,1:T(8,128)(2,1)}, u32[]{:S(2)}, u32[]{:S(2)}) async-start(bf16[2,16,48,2048]{3,2,0,1:T(8,128)(2,1)} %copy.50), calls=%async_computation.2 | async-start | bytes 12582912 | tf_op jit(solution)/shard_map/all_to_all | solution.py:70
  431.8 64.4 %all-gather.5.cloned.1.call-start = ((), (), s32[]{:S(2)}) async-start(), calls=%async_computation.9 | async-start | bytes 7077888 | tf_op jit(solution)/shard_map/all_gather | solution.py:95
  569.2 16.5 %slice-start = ((s8[6291456]{0:T(1024)(128)(4,1)}), s8[2097152]{0:T(1024)(128)(4,1)S(1)}, s32[]{:S(2)}) async-start(s8[6291456]{0:T(1024)(128)(4,1)} %bitcast.57), calls=%async_computation.10 | async-start | bytes 4194304
  569.2 142.7 %all-to-all-start.3 = ((bf16[2,16,48,2048]{3,2,0,1:T(8,128)(2,1)}), bf16[2,16,48,2048]{3,2,0,1:T(8,128)(2,1)}, u32[]{:S(2)}, u32[]{:S(2)}) async-start(bf16[2,16,48,2048]{3,2,0,1:T(8,128)(2,1)} %copy.56), calls=%async_computation.5 | async-start | bytes 12582912 | tf_op jit(solution)/shard_map/all_to_all | solution.py:105
  574.6 11.1 %slice-start.2 = ((s8[4718592]{0:T(1024)(128)(4,1)}), s8[4194304]{0:T(1024)(128)(4,1)S(1)}, s32[]{:S(2)}) async-start(s8[4718592]{0:T(1024)(128)(4,1)} %bitcast.69), calls=%async_computation.12 | async-start | bytes 8388608
  575.9 9.8 %slice-start.1 = ((s8[6291456]{0:T(1024)(128)(4,1)}), s8[4194304]{0:T(1024)(128)(4,1)S(1)}, s32[]{:S(2)}) async-start(s8[6291456]{0:T(1024)(128)(4,1)} %bitcast.57), calls=%async_computation.11 | async-start | bytes 8388608
  575.9 9.8 %slice-start.3 = ((s8[4718592]{0:T(1024)(128)(4,1)}), s8[524288]{0:T(1024)(128)(4,1)S(1)}, s32[]{:S(2)}) async-start(s8[4718592]{0:T(1024)(128)(4,1)} %bitcast.69), calls=%async_computation.13 | async-start | bytes 1048576
  604.7 22.4 %copy-start.4 = (f32[128,8]{1,0:T(8,128)S(1)}, f32[128,8]{1,0:T(8,128)}, u32[]{:S(2)}) copy-start(f32[128,8]{1,0:T(8,128)} %copy-done.3) | copy-start | bytes 12292
Sparse Core Ops, SparseCore 0:
  206.3 60.5 reduce-scatter.2
  338.6 34.1 reduce-scatter.4
  378.1 36.0 all-gather.2
  433.8 62.2 all-gather.4
where the time goes:
time: 752 us; the launch traced here: 744 us
  waiting for transfers between devices  493 us (66%)
  local copies, waits for them, and re-layouts  93.9 us (12%)
  matrix products  67.8 us (9%)
  other arithmetic  44.7 us (6%)
  starting transfers between devices  23.7 us (3%)
  between operations  14.5 us (2%)
    all_to_all x1, waiting for transfers between devices, local(): lax.all_to_all(grad_outbound.reshape(block_shape), 'expert', split_axis=1...  117 us
    all_to_all x1, waiting for transfers between devices, local(): lax.all_to_all(outbound.reshape(block_shape), 'expert', split_axis=1, con...  114 us
    all_to_all x1, waiting for transfers between devices, local(): lax.all_to_all(x_grad_slice.reshape(block_shape), 'expert', split_axis=1,...  77.4 us
    all_gather x1, waiting for transfers between devices, local(): preact_grad_all = lax.all_gather(preact_grad, 'dp', axis=0, tiled=True)  62.7 us
    all_to_all x1, waiting for transfers between devices, local(): lax.all_to_all(out_slice.reshape(block_shape), 'expert', split_axis=1, co...  55.4 us
    all_gather x1, waiting for transfers between devices, local(): hidden_all = lax.all_gather(hidden_mine, 'dp', axis=0, tiled=True)  36.2 us
    reduce_scatter x1, waiting for transfers between devices, local(): lax.psum_scatter(jnp.einsum('lrk,lfk->rlf', rows, down_weight, preferred_...  29.8 us
  transfers between devices with their start and end apart: 8, of which 7 were waited for; matrix products, arithmetic and copies ran while one was open for 17% of the time, Pallas kernels for 0%

commit v1 on v0

v1 whole, which is shorter than its diff:
```python
import jax
import jax.numpy as jnp
from jax import lax
from jax.sharding import PartitionSpec as P

BF16 = jnp.bfloat16
F32 = jnp.float32


def dot(a, b, contract):
    return lax.dot_general(a, b, (contract, ((), ())), preferred_element_type=F32)


def dp_sum(part):
    size = lax.axis_size("dp")
    if size == 2:
        other = lax.ppermute(part, "dp", [(0, 1), (1, 0)])
        return part.astype(F32) + other.astype(F32)
    return lax.psum(part.astype(F32), "dp")


def local(tokens, expert_ids, route_weights, gate_up_weight, down_weight, out_grad):
    tok_count, width = tokens.shape
    top_count = expert_ids.shape[1]
    groups = lax.axis_size("expert")
    local_count = gate_up_weight.shape[0]
    units = down_weight.shape[1]
    experts = local_count * groups
    capacity = 3 * tok_count * top_count // (2 * experts)
    rows = groups * capacity
    me = lax.axis_index("expert")

    routing = lax.all_gather(
        jnp.concatenate([expert_ids.astype(F32), route_weights], axis=1),
        "expert",
        axis=0,
        tiled=True,
    ).reshape(groups, tok_count, 2 * top_count)
    x_all = lax.all_gather(tokens, "expert", axis=0, tiled=True)
    og_all = lax.all_gather(out_grad, "expert", axis=0, tiled=True)
    x_all = x_all.reshape(groups, tok_count, width)
    og_all = og_all.reshape(groups, tok_count, width)

    ids = routing[..., :top_count]
    weights = routing[..., top_count:]
    mine = me * local_count + jnp.arange(local_count)
    hits = ids[None] == mine.astype(F32)[:, None, None, None]
    chosen = jnp.any(hits, axis=3)
    token_weight = jnp.sum(jnp.where(hits, weights[None], 0.0), axis=3)
    before = jnp.arange(tok_count)[:, None] < jnp.arange(tok_count)[None, :]
    rank = jnp.einsum(
        "lgt,tu->lgu", chosen.astype(BF16), before.astype(BF16), preferred_element_type=F32
    )
    places = jnp.arange(capacity, dtype=jnp.int32).astype(F32)
    picks = chosen[:, :, None, :] & (rank[:, :, None, :] == places[None, None, :, None])
    pick = picks.astype(BF16)
    slot_weight = jnp.sum(jnp.where(picks, token_weight[:, :, None, :], 0.0), axis=3)

    def slots(array, l):
        return (
            jnp.einsum("gct,gtd->gcd", pick[l], array, preferred_element_type=F32)
            .astype(BF16)
            .reshape(rows, width)
        )

    def combine(values):
        total = sum(
            jnp.einsum(
                "gct,gcd->gtd",
                pick[l],
                values[l].reshape(groups, capacity, width),
                preferred_element_type=F32,
            )
            for l in range(local_count)
        )
        return lax.psum_scatter(
            total.astype(BF16).reshape(groups * tok_count, width),
            "expert",
            scatter_dimension=0,
            tiled=True,
        )

    each = range(local_count)
    x_slots = [slots(x_all, l) for l in each]
    og_slots = [slots(og_all, l) for l in each]
    preact = [dp_sum(dot(x_slots[l], gate_up_weight[l], ((1,), (0,))).astype(BF16)) for l in each]
    raw_grad = [dp_sum(dot(og_slots[l], down_weight[l], ((1,), (1,))).astype(BF16)) for l in each]
    hidden_w, preact_grad, route_part = [], [], []
    for l in each:
        w = slot_weight[l].reshape(rows, 1)
        gate, up = preact[l][:, :units], preact[l][:, units:]
        sig = jax.nn.sigmoid(gate)
        act = gate * sig
        hidden = act * up
        hidden_w.append((w * hidden).astype(BF16))
        route_part.append(jnp.sum(hidden * raw_grad[l], axis=1).reshape(groups, capacity))
        grad = w * raw_grad[l]
        preact_grad.append(
            jnp.concatenate(
                [grad * up * sig * (1.0 + gate * (1.0 - sig)), grad * act], axis=1
            ).astype(BF16)
        )
    layer_out = combine([dot(hidden_w[l], down_weight[l], ((1,), (0,))).astype(BF16) for l in each])
    token_grad = combine(
        [dot(preact_grad[l], gate_up_weight[l], ((1,), (1,))).astype(BF16) for l in each]
    )
    gate_up_grad = jnp.stack(
        [dot(x_slots[l], preact_grad[l], ((0,), (0,))).astype(BF16) for l in each]
    )
    down_grad = jnp.stack([dot(hidden_w[l], og_slots[l], ((0,), (0,))).astype(BF16) for l in each])
    route_token = jnp.stack(
        [jnp.sum(jnp.where(picks[l], route_part[l][:, :, None], 0.0), axis=1) for l in each]
    )
    route_all = jnp.sum(jnp.where(hits, route_token[..., None], 0.0), axis=0)
    route_grad = lax.psum_scatter(
        route_all.reshape(groups * tok_count, top_count),
        "expert",
        scatter_dimension=0,
        tiled=True,
    )
    return layer_out, token_grad, route_grad, gate_up_grad, down_grad


def solution(mesh):
    placed = (
        P("expert", "dp"),
        P("expert", None),
        P("expert", None),
        P("expert", "dp", None),
        P("expert", None, "dp"),
        P("expert", "dp"),
    )
    return jax.shard_map(
        local,
        mesh=mesh,
        in_specs=placed,
        out_specs=(
            P("expert", "dp"),
            P("expert", "dp"),
            P("expert", None),
            P("expert", "dp", None),
            P("expert", None, "dp"),
        ),
        check_vma=False,
    )
```

time: 752 us -> 595 us (0.79)
  the two profiles are of different devices: /device:TPU:11 before, /device:TPU:0 now
where the time goes in v1:
time: 595 us; the launch traced here: 587 us
  waiting for transfers between devices  378 us (64%)
  matrix products  129 us (22%)
  other arithmetic  31.7 us (5%)
  blocking collectives  23.9 us (4%)
  between operations  14.5 us (2%)
    reduce_scatter x2, waiting for transfers between devices, combine(): lax.psum_scatter(total.astype(BF16).reshape(groups * tok_count, width), '...  185 us
    ppermute x4, waiting for transfers between devices, dp_sum(): other = lax.ppermute(part, 'dp', [(0, 1), (1, 0)])  80.7 us
    dot_general x12, matrix products, dot(): lax.dot_general(a, b, (contract, ((), ())), preferred_element_type=F32)  74.5 us
    all_gather x1, waiting for transfers between devices, local(): og_all = lax.all_gather(out_grad, 'expert', axis=0, tiled=True)  57.7 us
    all_gather x1, waiting for transfers between devices, local(): x_all = lax.all_gather(tokens, 'expert', axis=0, tiled=True)  53.5 us
    dot_general x4, matrix products, combine(): jnp.einsum('gct,gcd->gtd', pick[l], values[l].reshape(groups, capacity, w...  40.2 us
    all_gather x1, blocking collectives, local(): lax.all_gather(jnp.concatenate([expert_ids.astype(F32), route_weights], a...  23.9 us
    dot_general x4, matrix products, slots(): jnp.einsum('gct,gtd->gcd', pick[l], array, preferred_element_type=F32)  13.6 us
  transfers between devices with their start and end apart: 9, of which 7 were waited for; matrix products, arithmetic and copies ran while one was open for 22% of the time, Pallas kernels for 0%

profile of v1, /device:TPU:0, one launch (start us, length us, event | category | flops | bytes accessed | tf_op | source)
XLA Modules:
  0.0 587.0 jit_solution(6516776161546111398)
XLA Ops:
  7.2 0.7 all-gather.3.cloned.1.call-update
  7.9 0.7 all-gather.5.cloned.1.call-update
  8.7 0.7 convert_element_type.106
  9.4 0.7 pad_maximum_fusion.9
  10.1 23.9 %all_gather.9 = f32[2048,16]{0,1:T(8,128)S(1)} all-gather(f32[128,16]{0,1:T(8,128)S(1)} %pad_maximum_fusion.9), channel_id=1, replica_groups=mesh['dp'=2,'expert'=16] {'expert'}, dimensions={0}, use_global_device_ids=true | all-gather | bytes 139264 | tf_op jit(solution)/shard_map/all_gather | solution.py:33
  34.6 53.5 %all-gather.3.cloned.1.call-done = bf16[2048,2048]{1,0:T(8,128)(2,1)} async-done(((bf16[128,2048]{1,0:T(8,128)(2,1)}), bf16[2048,2048]{1,0:T(8,128)(2,1)}) %all-gather.3.cloned.1.call-update) | async-done | bytes 8388624 | tf_op jit(solution)/shard_map/all_gather | solution.py:39
  88.1 4.8 convolution_convert_fusion.9
  92.8 2.2 copy-done.18
  95.0 6.3 %fusion.14 = bf16[768,1536]{1,0:T(8,128)(2,1)} fusion(bf16[768,2048]{1,0:T(8,128)(2,1)S(1)} %bitcast.111, bf16[2,2048,1536]{2,1,0:T(8,128)(2,1)S(1)} %copy-done.18), kind=kOutput, calls=%fused_computation.22 | convolution fusion | flops 4833017856 | bytes 11796480 | tf_op jit(solution)/shard_map/dot_general | solution.py:11
  101.3 1.5 collective-permute-start
  102.8 2.9 convolution_convert_fusion.7
  105.7 57.7 %all-gather.5.cloned.1.call-done = bf16[2048,2048]{1,0:T(8,128)(2,1)} async-done(((bf16[128,2048]{1,0:T(8,128)(2,1)}), bf16[2048,2048]{1,0:T(8,128)(2,1)}) %all-gather.5.cloned.1.call-update) | async-done | bytes 8388624 | tf_op jit(solution)/shard_map/all_gather | solution.py:40
  163.4 4.8 convolution_convert_fusion.5
  168.2 5.7 fusion.42
  174.0 1.5 collective-permute-start.2
  175.6 6.5 %fusion.17 = bf16[768,1536]{1,0:T(8,128)(2,1)} fusion(bf16[768,2048]{1,0:T(8,128)(2,1)S(1)} %bitcast.113, bf16[2,2048,1536]{2,1,0:T(8,128)(2,1)S(1)} %bitcast.127), kind=kOutput, calls=%fused_computation.23 | convolution fusion | flops 4833017856 | bytes 11796480 | tf_op jit(solution)/shard_map/dot_general | solution.py:11
  182.1 0.6 collective-permute-start.1
  182.7 1.2 convolution_convert_fusion.4
  184.0 3.7 fusion.45
  187.7 1.5 collective-permute-start.3
  189.2 3.1 convert_add_fusion.1
  192.2 10.6 %collective-permute-done.2 = bf16[768,768]{1,0:T(8,128)(2,1)S(1)} collective-permute-done((bf16[768,768]{1,0:T(8,128)(2,1)S(1)}, bf16[768,768]{1,0:T(8,128)(2,1)S(1)}, u32[]{:S(2)}, u32[]{:S(2)}) %collective-permute-start.2) | collective-permute-done | bytes 1179680 | tf_op jit(solution)/shard_map/ppermute | solution.py:17
  202.9 1.0 copy-done.8
  203.9 1.0 multiply_reduce_fusion.1
  204.9 48.6 %collective-permute-done.1 = bf16[768,1536]{1,0:T(8,128)(2,1)} collective-permute-done((bf16[768,1536]{1,0:T(8,128)(2,1)}, bf16[768,1536]{1,0:T(8,128)(2,1)}, u32[]{:S(2)}, u32[]{:S(2)}) %collective-permute-start.1) | collective-permute-done | bytes 2359328 | tf_op jit(solution)/shard_map/ppermute | solution.py:17
  253.5 3.1 convert_add_fusion
  256.6 21.5 %collective-permute-done.3 = bf16[768,768]{1,0:T(8,128)(2,1)} collective-permute-done((bf16[768,768]{1,0:T(8,128)(2,1)}, bf16[768,768]{1,0:T(8,128)(2,1)}, u32[]{:S(2)}, u32[]{:S(2)}) %collective-permute-start.3) | collective-permute-done | bytes 1179680 | tf_op jit(solution)/shard_map/ppermute | solution.py:17
  278.1 2.5 multiply_reduce_fusion
  281.0 0.7 fusion.49
  282.2 4.9 multiply_convert_fusion.3
  287.1 5.1 convolution_convert_fusion.8
  292.3 8.1 %fusion.54 = f32[16,128,2048]{2,1,0:T(8,128)} fusion(bf16[16,48,2048]{2,1,0:T(8,128)(2,1)S(1)} %bitcast.109, pred[2,16,48,128]{3,2,1,0:T(8,128)(4,1)S(1)} %compare_and_fusion), kind=kOutput, calls=%fused_computation.83 | convolution fusion | flops 402653184 | bytes 20021248 | tf_op jit(solution)/shard_map/gct,gcd->gtd/dot_general | solution.py:68
  300.5 4.9 multiply_convert_fusion.1
  305.3 6.3 %convolution_convert_fusion.6 = bf16[768,2048]{1,0:T(8,128)(2,1)} fusion(bf16[768,768]{1,0:T(8,128)(2,1)S(1)} %get-tuple-element.13, bf16[2,768,2048]{2,1,0:T(8,128)(2,1)} %param.10), kind=kOutput, calls=%fused_computation.28 | convolution fusion | flops 2417491968 | bytes 7471104 | tf_op jit(solution)/shard_map/dot_general | solution.py:11
  311.7 12.4 %add_convert_fusion.1 = bf16[16,128,2048]{2,1,0:T(8,128)(2,1)} fusion(f32[16,128,2048]{2,1,0:T(8,128)} %fusion.54, bf16[16,48,2048]{2,1,0:T(8,128)(2,1)} %bitcast.119, pred[2,16,48,128]{3,2,1,0:T(8,128)(4,1)S(1)} %compare_and_fusion), kind=kOutput, calls=%fused_computation.1 | convolution fusion | flops 411041792 | bytes 28409856 | tf_op jit(solution)/shard_map/gct,gcd->gtd/dot_general | solution.py:68
  324.2 16.2 %fusion.20 = bf16[768,2048]{1,0:T(8,128)(2,1)S(1)} fusion(bf16[2,2048,1536]{2,1,0:T(8,128)(2,1)} %param.9, bf16[768,768]{1,0:T(8,128)(2,1)} %get-tuple-element.12, bf16[768,768]{1,0:T(8,128)(2,1)} %get-tuple-element.11), kind=kOutput, calls=%fused_computation.32 | convolution fusion | flops 4838129664 | bytes 11796480 | tf_op jit(solution)/shard_map/dot_general | solution.py:11
  340.5 8.1 %fusion.53 = f32[16,128,2048]{2,1,0:T(8,128)} fusion(bf16[16,48,2048]{2,1,0:T(8,128)(2,1)S(1)} %bitcast.110, pred[2,16,48,128]{3,2,1,0:T(8,128)(4,1)S(1)} %compare_and_fusion), kind=kOutput, calls=%fused_computation.82 | convolution fusion | flops 402653184 | bytes 20021248 | tf_op jit(solution)/shard_map/gct,gcd->gtd/dot_general | solution.py:68
  348.6 5.3 fusion.23
  353.9 11.5 %add_convert_fusion = bf16[16,128,2048]{2,1,0:T(8,128)(2,1)} fusion(f32[16,128,2048]{2,1,0:T(8,128)} %fusion.53, bf16[16,48,2048]{2,1,0:T(8,128)(2,1)S(1)} %bitcast.120, pred[2,16,48,128]{3,2,1,0:T(8,128)(4,1)S(1)} %compare_and_fusion), kind=kOutput, calls=%fused_computation | convolution fusion | flops 411041792 | bytes 28409856 | tf_op jit(solution)/shard_map/gct,gcd->gtd/dot_general | solution.py:68
  365.5 5.0 fusion.33
  370.6 2.9 fusion.32
  373.5 4.0 pad_maximum_fusion.1
  377.5 1.0 copy-done.14
  378.9 5.9 %fusion.1 = bf16[1,2048,1536]{2,1,0:T(8,128)(2,1)S(1)} fusion(bf16[768,2048]{1,0:T(8,128)(2,1)S(1)} %bitcast.114, bf16[768,768]{1,0:T(8,128)(2,1)S(1)} %copy-done.16, bf16[768,768]{1,0:T(8,128)(2,1)S(1)} %copy-done.14), kind=kOutput, calls=%fused_computation.6 | convolution fusion | flops 4839702528 | bytes 11796480 | tf_op jit(solution)/shard_map/dot_general | solution.py:11
  384.8 5.6 fusion
  390.4 5.2 pad_maximum_fusion
  395.6 75.1 %reduce-scatter.4.cloned.1.call-done = bf16[128,2048]{1,0:T(8,128)(2,1)} async-done(((bf16[2048,2048]{1,0:T(8,128)(2,1)}), bf16[128,2048]{1,0:T(8,128)(2,1)}) %reduce-scatter.4.cloned.1.call-update) | async-done | bytes 524304 | tf_op jit(solution)/shard_map/reduce_scatter | solution.py:76
  470.7 109.5 %reduce-scatter.6.cloned.1.call-done = bf16[128,2048]{1,0:T(8,128)(2,1)} async-done(((bf16[2048,2048]{1,0:T(8,128)(2,1)}), bf16[128,2048]{1,0:T(8,128)(2,1)}) %reduce-scatter.6.cloned.1.call-update) | async-done | bytes 524304 | tf_op jit(solution)/shard_map/reduce_scatter | solution.py:76
  (91 shorter events, 2.4 us)
Async XLA Ops:
  7.2 80.9 %all-gather.3.cloned.1.call-start = ((), (), s32[]{:S(2)}) async-start(), calls=%async_computation.3 | async-start | bytes 8912896 | tf_op jit(solution)/shard_map/all_gather | solution.py:39
  7.9 155.5 %all-gather.5.cloned.1.call-start = ((), (), s32[]{:S(2)}) async-start(), calls=%async_computation.5 | async-start | bytes 8912896 | tf_op jit(solution)/shard_map/all_gather | solution.py:40
  8.6 387.0 %reduce-scatter.8.cloned.1.call-start = ((), (), s32[]{:S(2)}) async-start(), calls=%async_computation.7 | async-start | bytes 69632 | tf_op jit(solution)/shard_map/reduce_scatter | solution.py:115
  88.0 7.0 %copy-start.18 = (bf16[2,2048,1536]{2,1,0:T(8,128)(2,1)S(1)}, bf16[2,2048,1536]{2,1,0:T(8,128)(2,1)}, u32[]{:S(2)}) copy-start(bf16[2,2048,1536]{2,1,0:T(8,128)(2,1)} %param.9) | copy-start | bytes 37748740
  88.0 14.7 %slice-start.2 = ((s8[8388608]{0:T(1024)(128)(4,1)}), s8[4194304]{0:T(1024)(128)(4,1)S(1)}, s32[]{:S(2)}) async-start(s8[8388608]{0:T(1024)(128)(4,1)} %bitcast.104), calls=%async_computation.10 | async-start | bytes 8388608
  95.0 7.7 %slice-start.3 = ((s8[8388608]{0:T(1024)(128)(4,1)}), s8[4194304]{0:T(1024)(128)(4,1)S(1)}, s32[]{:S(2)}) async-start(s8[8388608]{0:T(1024)(128)(4,1)} %bitcast.104), calls=%async_computation.11 | async-start | bytes 8388608
  101.3 87.9 %collective-permute-start = (bf16[768,1536]{1,0:T(8,128)(2,1)}, bf16[768,1536]{1,0:T(8,128)(2,1)}, u32[]{:S(2)}, u32[]{:S(2)}) collective-permute-start(bf16[768,1536]{1,0:T(8,128)(2,1)} %fusion.14), channel_id=1, source_target_pairs={{0,16},{16,0},{1,17},{17,1},{2,18},{18,2},{3,19},{19,3},{4,20},{20... | collective-permute-start | bytes 7077896 | tf_op jit(solution)/shard_map/ppermute | solution.py:17
  163.4 12.1 %slice-start.4 = ((s8[12582912]{0:T(1024)(128)(4,1)}), s8[4194304]{0:T(1024)(128)(4,1)S(1)}, s32[]{:S(2)}) async-start(s8[12582912]{0:T(1024)(128)(4,1)} %bitcast.126), calls=%async_computation.12 | async-start | bytes 8388608
  163.4 12.1 %slice-start.5 = ((s8[12582912]{0:T(1024)(128)(4,1)}), s8[4194304]{0:T(1024)(128)(4,1)S(1)}, s32[]{:S(2)}) async-start(s8[12582912]{0:T(1024)(128)(4,1)} %bitcast.126), calls=%async_computation.13 | async-start | bytes 8388608
  168.2 5.8 copy-start.4
  168.2 7.4 %copy-start.2 = (bf16[16,48,2048]{2,1,0:T(8,128)(2,1)S(1)}, bf16[16,48,2048]{2,1,0:T(8,128)(2,1)}, u32[]{:S(2)}) copy-start(bf16[16,48,2048]{2,1,0:T(8,128)(2,1)} %convolution_convert_fusion.7) | copy-start | bytes 9437188
  168.2 7.3 %slice-start.6 = ((s8[12582912]{0:T(1024)(128)(4,1)}), s8[4194304]{0:T(1024)(128)(4,1)S(1)}, s32[]{:S(2)}) async-start(s8[12582912]{0:T(1024)(128)(4,1)} %bitcast.126), calls=%async_computation.14 | async-start | bytes 8388608
  168.2 14.5 %slice-start = ((s8[8388608]{0:T(1024)(128)(4,1)}), s8[4194304]{0:T(1024)(128)(4,1)S(1)}, s32[]{:S(2)}) async-start(s8[8388608]{0:T(1024)(128)(4,1)} %bitcast.100), calls=%async_computation.8 | async-start | bytes 8388608
  168.2 15.8 %slice-start.10 = ((s8[6291456]{0:T(1024)(128)(4,1)}), s8[4194304]{0:T(1024)(128)(4,1)S(1)}, s32[]{:S(2)}) async-start(s8[6291456]{0:T(1024)(128)(4,1)} %bitcast.130), calls=%async_computation.18 | async-start | bytes 8388608
  174.0 28.9 %copy-start.7 = (bf16[768,768]{1,0:T(8,128)(2,1)}, bf16[768,768]{1,0:T(8,128)(2,1)S(1)}, u32[]{:S(2)}) copy-start(bf16[768,768]{1,0:T(8,128)(2,1)S(1)} %fusion.42) | copy-start | bytes 3538948
  174.0 28.9 %collective-permute-start.2 = (bf16[768,768]{1,0:T(8,128)(2,1)S(1)}, bf16[768,768]{1,0:T(8,128)(2,1)S(1)}, u32[]{:S(2)}, u32[]{:S(2)}) collective-permute-start(bf16[768,768]{1,0:T(8,128)(2,1)S(1)} %fusion.42), channel_id=1, source_target_pairs={{0,16},{16,0},{1,17},{17,1},{2,18},{18,2},{3,19},{19,3},{4,20},{20... | collective-permute-start | bytes 3538952 | tf_op jit(solution)/shard_map/ppermute | solution.py:17
  175.5 7.2 %slice-start.1 = ((s8[8388608]{0:T(1024)(128)(4,1)}), s8[4194304]{0:T(1024)(128)(4,1)S(1)}, s32[]{:S(2)}) async-start(s8[8388608]{0:T(1024)(128)(4,1)} %bitcast.100), calls=%async_computation.9 | async-start | bytes 8388608
  175.5 8.4 %slice-start.11 = ((s8[6291456]{0:T(1024)(128)(4,1)}), s8[2097152]{0:T(1024)(128)(4,1)S(1)}, s32[]{:S(2)}) async-start(s8[6291456]{0:T(1024)(128)(4,1)} %bitcast.130), calls=%async_computation.19 | async-start | bytes 4194304
  182.1 71.4 %collective-permute-start.1 = (bf16[768,1536]{1,0:T(8,128)(2,1)}, bf16[768,1536]{1,0:T(8,128)(2,1)}, u32[]{:S(2)}, u32[]{:S(2)}) collective-permute-start(bf16[768,1536]{1,0:T(8,128)(2,1)} %fusion.17), channel_id=1, source_target_pairs={{0,16},{16,0},{1,17},{17,1},{2,18},{18,2},{3,19},{19,3},{4,20},{20... | collective-permute-start | bytes 7077896 | tf_op jit(solution)/shard_map/ppermute | solution.py:17
  183.9 3.7 copy-start.6
  187.7 90.4 %collective-permute-start.3 = (bf16[768,768]{1,0:T(8,128)(2,1)}, bf16[768,768]{1,0:T(8,128)(2,1)}, u32[]{:S(2)}, u32[]{:S(2)}) collective-permute-start(bf16[768,768]{1,0:T(8,128)(2,1)} %fusion.45), channel_id=1, source_target_pairs={{0,16},{16,0},{1,17},{17,1},{2,18},{18,2},{3,19},{19,3},{4,20},{20... | collective-permute-start | bytes 3538952 | tf_op jit(solution)/shard_map/ppermute | solution.py:17
  192.2 10.6 %copy-start.1 = (f32[768,1536]{1,0:T(8,128)}, f32[768,1536]{1,0:T(8,128)S(1)}, u32[]{:S(2)}) copy-start(f32[768,1536]{1,0:T(8,128)S(1)} %convert_add_fusion.1) | copy-start | bytes 14155780
  202.8 1.0 copy-start.8
  256.6 21.6 %copy-start = (f32[768,1536]{1,0:T(8,128)}, f32[768,1536]{1,0:T(8,128)S(1)}, u32[]{:S(2)}) copy-start(f32[768,1536]{1,0:T(8,128)S(1)} %convert_add_fusion) | copy-start | bytes 14155780
  287.1 5.1 copy-start.11
  305.3 6.3 %copy-start.17 = (bf16[768,768]{1,0:T(8,128)(2,1)}, bf16[768,768]{1,0:T(8,128)(2,1)S(1)}, u32[]{:S(2)}) copy-start(bf16[768,768]{1,0:T(8,128)(2,1)S(1)} %get-tuple-element.13) | copy-start | bytes 3538948
  311.6 159.1 %reduce-scatter.4.cloned.1.call-start = ((), (), s32[]{:S(2)}) async-start(), calls=%async_computation.4 | async-start | bytes 8912896 | tf_op jit(solution)/shard_map/reduce_scatter | solution.py:76
  324.1 256.1 %reduce-scatter.6.cloned.1.call-start = ((), (), s32[]{:S(2)}) async-start(), calls=%async_computation.6 | async-start | bytes 8912896 | tf_op jit(solution)/shard_map/reduce_scatter | solution.py:76
  324.2 24.4 %slice-start.7 = ((s8[12582912]{0:T(1024)(128)(4,1)}), s8[4194304]{0:T(1024)(128)(4,1)S(1)}, s32[]{:S(2)}) async-start(s8[12582912]{0:T(1024)(128)(4,1)} %bitcast.128), calls=%async_computation.15 | async-start | bytes 8388608
  324.2 24.4 %slice-start.8 = ((s8[12582912]{0:T(1024)(128)(4,1)}), s8[4194304]{0:T(1024)(128)(4,1)S(1)}, s32[]{:S(2)}) async-start(s8[12582912]{0:T(1024)(128)(4,1)} %bitcast.128), calls=%async_computation.16 | async-start | bytes 8388608
  340.4 8.2 %copy-start.13 = (bf16[768,768]{1,0:T(8,128)(2,1)S(1)}, bf16[768,768]{1,0:T(8,128)(2,1)}, u32[]{:S(2)}) copy-start(bf16[768,768]{1,0:T(8,128)(2,1)} %get-tuple-element.9) | copy-start | bytes 3538948
  340.5 8.2 %copy-start.15 = (bf16[768,768]{1,0:T(8,128)(2,1)S(1)}, bf16[768,768]{1,0:T(8,128)(2,1)}, u32[]{:S(2)}) copy-start(bf16[768,768]{1,0:T(8,128)(2,1)} %get-tuple-element.10) | copy-start | bytes 3538948
  340.5 8.2 %slice-start.9 = ((s8[12582912]{0:T(1024)(128)(4,1)}), s8[4194304]{0:T(1024)(128)(4,1)S(1)}, s32[]{:S(2)}) async-start(s8[12582912]{0:T(1024)(128)(4,1)} %bitcast.128), calls=%async_computation.17 | async-start | bytes 8388608
  365.5 5.1 copy-start.5
  365.5 5.1 copy-start.12
  373.5 4.0 copy-start.3
  373.5 4.9 copy-start.14
  373.5 5.4 copy-start.16
  378.9 5.9 %copy-start.9 = (bf16[768,768]{1,0:T(8,128)(2,1)S(1)}, bf16[768,768]{1,0:T(8,128)(2,1)}, u32[]{:S(2)}) copy-start(bf16[768,768]{1,0:T(8,128)(2,1)} %get-tuple-element.11) | copy-start | bytes 3538948
  378.9 5.9 %copy-start.10 = (bf16[768,768]{1,0:T(8,128)(2,1)S(1)}, bf16[768,768]{1,0:T(8,128)(2,1)}, u32[]{:S(2)}) copy-start(bf16[768,768]{1,0:T(8,128)(2,1)} %get-tuple-element.12) | copy-start | bytes 3538948
Sparse Core Ops, SparseCore 0:
  10.2 77.8 all-gather.2
  90.2 73.1 all-gather.4
  311.7 50.1 reduce-scatter.7
  366.9 103.7 reduce-scatter.3
  475.7 104.4 reduce-scatter.5

commit v2 on v1

--- a/solution.py
+++ b/solution.py
@@ -17,6 +17,77 @@
         other = lax.ppermute(part, "dp", [(0, 1), (1, 0)])
         return part.astype(F32) + other.astype(F32)
     return lax.psum(part.astype(F32), "dp")
+
+
+def ring_step(axis_size, step):
+    chips = axis_size // 2
+    order = [2 * i if 2 * i < chips else 2 * (chips - 1 - i) + 1 for i in range(chips)]
+    return [
+        (2 * order[i] + core, 2 * order[(i + step) % chips] + core)
+        for i in range(chips)
+        for core in range(2)
+    ]
+
+
+def move(array, step):
+    return lax.ppermute(array, "expert", ring_step(lax.axis_size("expert"), step))
+
+
+def swap(array):
+    size = lax.axis_size("expert")
+    return lax.ppermute(array, "expert", [(i, i ^ 1) for i in range(size)])
+
+
+def hops(more):
+    chips = lax.axis_size("expert") // 2
+    return (chips // 2, chips - 1 - chips // 2) if more else (chips - 1 - chips // 2, chips // 2)
+
+
+def after(array, earlier):
+    return lax.optimization_barrier((array, earlier))[0]
+
+
+def gather_ring(shard, more, behind=None):
+    chips = lax.axis_size("expert") // 2
+    ahead, back = hops(more)
+    held = [None] * chips
+    held[0] = shard
+    first = shard if behind is None else after(shard, behind[0])
+    second = shard if behind is None else after(shard, behind[1])
+    for hop in range(1, max(ahead, back) + 1):
+        if hop <= ahead:
+            first = move(first, 1)
+            held[hop] = first
+        if hop <= back:
+            second = move(second, -1)
+            held[chips - hop] = second
+    return jnp.stack(held + [swap(piece) for piece in held]), (first, second)
+
+
+def scatter_ring(parts, more):
+    chips = parts.shape[0] // 2
+    ahead, back = hops(more)
+    paired = swap(parts[chips:])
+
+    def mine(o):
+        return parts[o].astype(F32) + paired[o].astype(F32)
+
+    first, second = mine(chips - ahead), mine(back)
+    for hop in range(max(ahead, back) - 1, -1, -1):
+        if hop < ahead:
+            first = move(first.astype(BF16), 1).astype(F32)
+            if hop:
+                first = first + mine(chips - hop)
+        if hop < back:
+            second = move(second.astype(BF16), -1).astype(F32)
+            if hop:
+                second = second + mine(hop)
+    return (mine(0) + first + second).astype(BF16)
+
+
+def reorder(array, index):
+    pick = index[:, None] == jnp.arange(array.shape[0])[None, :]
+    return jnp.sum(jnp.where(pick[:, :, None, None], array[None], 0.0), axis=1)
 
 
 def local(tokens, expert_ids, route_weights, gate_up_weight, down_weight, out_grad):
@@ -30,16 +101,24 @@
     rows = groups * capacity
     me = lax.axis_index("expert")
 
+    chips = groups // 2
+    spot = jnp.arange(groups)
+    place = jnp.where(spot // 2 % 2 == 0, spot // 4, chips - 1 - spot // 4)
+    my_place = jnp.where(me // 2 % 2 == 0, me // 4, chips - 1 - me // 4)
+    where = (my_place - place) % chips + jnp.where(spot % 2 == me % 2, 0, chips)
+    chip_at = (my_place - spot % chips) % chips
+    chip_at = jnp.where(2 * chip_at < chips, 2 * chip_at, 2 * (chips - 1 - chip_at) + 1)
+    order = 2 * chip_at + (me % 2 + spot // chips) % 2
+
+    x_all, ends = gather_ring(tokens, True)
+    og_all, _ = gather_ring(out_grad, False, ends)
     routing = lax.all_gather(
         jnp.concatenate([expert_ids.astype(F32), route_weights], axis=1),
         "expert",
         axis=0,
         tiled=True,
     ).reshape(groups, tok_count, 2 * top_count)
-    x_all = lax.all_gather(tokens, "expert", axis=0, tiled=True)
-    og_all = lax.all_gather(out_grad, "expert", axis=0, tiled=True)
-    x_all = x_all.reshape(groups, tok_count, width)
-    og_all = og_all.reshape(groups, tok_count, width)
+    routing = reorder(routing, order)
 
     ids = routing[..., :top_count]
     weights = routing[..., top_count:]
@@ -63,7 +142,7 @@
             .reshape(rows, width)
         )
 
-    def combine(values):
+    def combine(values, more):
         total = sum(
             jnp.einsum(
                 "gct,gcd->gtd",
@@ -73,12 +152,7 @@
             )
             for l in range(local_count)
         )
-        return lax.psum_scatter(
-            total.astype(BF16).reshape(groups * tok_count, width),
-            "expert",
-            scatter_dimension=0,
-            tiled=True,
-        )
+        return scatter_ring(total.astype(BF16), more)
 
     each = range(local_count)
     x_slots = [slots(x_all, l) for l in each]
@@ -100,9 +174,11 @@
                 [grad * up * sig * (1.0 + gate * (1.0 - sig)), grad * act], axis=1
             ).astype(BF16)
         )
-    layer_out = combine([dot(hidden_w[l], down_weight[l], ((1,), (0,))).astype(BF16) for l in each])
+    layer_out = combine(
+        [dot(hidden_w[l], down_weight[l], ((1,), (0,))).astype(BF16) for l in each], True
+    )
     token_grad = combine(
-        [dot(preact_grad[l], gate_up_weight[l], ((1,), (1,))).astype(BF16) for l in each]
+        [dot(preact_grad[l], gate_up_weight[l], ((1,), (1,))).astype(BF16) for l in each], False
     )
     gate_up_grad = jnp.stack(
         [dot(x_slots[l], preact_grad[l], ((0,), (0,))).astype(BF16) for l in each]
@@ -112,6 +188,7 @@
         [jnp.sum(jnp.where(picks[l], route_part[l][:, :, None], 0.0), axis=1) for l in each]
     )
     route_all = jnp.sum(jnp.where(hits, route_token[..., None], 0.0), axis=0)
+    route_all = reorder(route_all, where)
     route_grad = lax.psum_scatter(
         route_all.reshape(groups * tok_count, top_count),
         "expert",

time: 595 us -> 490 us (0.82)
  waiting for transfers between devices: 378 us -> 205 us
  starting transfers between devices: 5.29 us -> 35.4 us
  local copies, waits for them, and re-layouts: 5.19 us -> 29.7 us
  other arithmetic: 31.7 us -> 55.3 us
  matrix products: 129 us -> 117 us
    reduce_scatter x2 -> x0, waiting for transfers between devices: 185 us -> none  [combine(): lax.psum_scatter(total.astype(BF16).reshape(groups * tok_count, width), '...]
    all_gather x2 -> x0, waiting for transfers between devices: 111 us -> none  [the longest x1 57.7 us: local(): og_all = lax.all_gather(out_grad, 'expert', axis=0, tiled=True)]
    ppermute x0 -> x46, waiting for transfers between devices: none -> 107 us  [the longest x28 102 us: move(): lax.ppermute(array, 'expert', ring_step(lax.axis_size('expert'), step))]
    ppermute x0 -> x46, starting transfers between devices: none -> 31.1 us  [the longest x28 27.9 us: move(): lax.ppermute(array, 'expert', ring_step(lax.axis_size('expert'), step))]
    convert_element_type x0 -> x10, other arithmetic: none -> 18.8 us  [the longest x7 13.2 us: scatter_ring(): first = move(first.astype(BF16), 1).astype(F32)]
    unnamed x65 -> x98, local copies, waits for them, and re-layouts: 4.88 us -> 23.1 us
    ppermute x4, waiting for transfers between devices: 80.7 us -> 98.1 us  [dp_sum(): other = lax.ppermute(part, 'dp', [(0, 1), (1, 0)])]
  transfers between devices with their start and end apart: 9 -> 51, of which waited for: 7 -> 25; matrix products, arithmetic and copies ran while one was open for 22% -> 31% of each run, Pallas kernels for 0% -> 0%
where the time goes in v2:
time: 490 us; the launch traced here: 482 us
  waiting for transfers between devices  205 us (42%)
  matrix products  117 us (24%)
  other arithmetic  55.3 us (11%)
  starting transfers between devices  35.4 us (7%)
  local copies, waits for them, and re-layouts  29.7 us (6%)
  blocking collectives  23.8 us (5%)
  between operations  15.3 us (3%)
    ppermute x28, waiting for transfers between devices, move(): lax.ppermute(array, 'expert', ring_step(lax.axis_size('expert'), step))  102 us
    ppermute x4, waiting for transfers between devices, dp_sum(): other = lax.ppermute(part, 'dp', [(0, 1), (1, 0)])  98.1 us
    dot_general x12, matrix products, dot(): lax.dot_general(a, b, (contract, ((), ())), preferred_element_type=F32)  73.7 us
    dot_general x4, matrix products, combine(): jnp.einsum('gct,gcd->gtd', pick[l], values[l].reshape(groups, capacity, w...  34.6 us
    ppermute x28, starting transfers between devices, move(): lax.ppermute(array, 'expert', ring_step(lax.axis_size('expert'), step))  27.9 us
    all_gather x1, blocking collectives, local(): lax.all_gather(jnp.concatenate([expert_ids.astype(F32), route_weights], a...  23.8 us
    unnamed x98, local copies, waits for them, and re-layouts  23.1 us
    convert_element_type x7, other arithmetic, scatter_ring(): first = move(first.astype(BF16), 1).astype(F32)  13.2 us
  transfers between devices with their start and end apart: 51, of which 25 were waited for; matrix products, arithmetic and copies ran while one was open for 31% of the time, Pallas kernels for 0%

profile of v2, /device:TPU:0, one launch (start us, length us, event | category | flops | bytes accessed | tf_op | source)
XLA Modules:
  0.0 481.6 jit_solution(10736580942261136263)
XLA Ops:
  7.2 3.1 collective-permute-start
  14.1 23.8 %all_gather.3 = f32[2048,16]{0,1:T(8,128)S(1)} all-gather(f32[128,16]{0,1:T(8,128)S(1)} %pad_maximum_fusion.9), channel_id=1, replica_groups=mesh['dp'=2,'expert'=16] {'expert'}, dimensions={0}, use_global_device_ids=true | all-gather | bytes 139264 | tf_op jit(solution)/shard_map/all_gather | solution.py:115
  42.2 11.8 %collective-permute-done.1 = bf16[128,2048]{1,0:T(8,128)(2,1)S(1)} collective-permute-done((bf16[128,2048]{1,0:T(8,128)(2,1)S(1)}, bf16[128,2048]{1,0:T(8,128)(2,1)S(1)}, u32[]{:S(2)}, u32[]{:S(2)}) %collective-permute-start.1) | collective-permute-done | bytes 524320 | tf_op jit(solution)/shard_map/ppermute | solution.py:33
  57.0 10.3 %collective-permute-done.2 = bf16[128,2048]{1,0:T(8,128)(2,1)S(1)} collective-permute-done((bf16[128,2048]{1,0:T(8,128)(2,1)S(1)}, bf16[128,2048]{1,0:T(8,128)(2,1)S(1)}, u32[]{:S(2)}, u32[]{:S(2)}) %collective-permute-start.2) | collective-permute-done | bytes 524320 | tf_op jit(solution)/shard_map/ppermute | solution.py:33
  69.6 10.2 %collective-permute-done.3 = bf16[128,2048]{1,0:T(8,128)(2,1)S(1)} collective-permute-done((bf16[128,2048]{1,0:T(8,128)(2,1)S(1)}, bf16[128,2048]{1,0:T(8,128)(2,1)S(1)}, u32[]{:S(2)}, u32[]{:S(2)}) %collective-permute-start.3) | collective-permute-done | bytes 524320 | tf_op jit(solution)/shard_map/ppermute | solution.py:33
  90.3 7.1 %collective-permute-done.28 = bf16[128,2048]{1,0:T(8,128)(2,1)S(1)} collective-permute-done((bf16[128,2048]{1,0:T(8,128)(2,1)S(1)}, bf16[128,2048]{1,0:T(8,128)(2,1)S(1)}, u32[]{:S(2)}, u32[]{:S(2)}) %collective-permute-start.28) | collective-permute-done | bytes 524320 | tf_op jit(solution)/shard_map/ppermute | solution.py:33
  100.2 4.6 convolution_convert_fusion.9
  104.9 9.2 %fusion.14 = bf16[768,1536]{1,0:T(8,128)(2,1)S(1)} fusion(bf16[768,2048]{1,0:T(8,128)(2,1)S(1)} %bitcast.228, bf16[2,2048,1536]{2,1,0:T(8,128)(2,1)} %param.9), kind=kOutput, calls=%fused_computation.22 | convolution fusion | flops 4833017856 | bytes 11796480 | tf_op jit(solution)/shard_map/dot_general | solution.py:11
  119.0 8.8 %fusion.17 = bf16[768,1536]{1,0:T(8,128)(2,1)S(1)} fusion(bf16[768,2048]{1,0:T(8,128)(2,1)S(1)} %bitcast.230, bf16[2,2048,1536]{2,1,0:T(8,128)(2,1)} %param.9), kind=kOutput, calls=%fused_computation.23 | convolution fusion | flops 4833017856 | bytes 11796480 | tf_op jit(solution)/shard_map/dot_general | solution.py:11
  133.3 9.7 %collective-permute-done.27 = bf16[128,2048]{1,0:T(8,128)(2,1)S(1)} collective-permute-done((bf16[128,2048]{1,0:T(8,128)(2,1)S(1)}, bf16[128,2048]{1,0:T(8,128)(2,1)S(1)}, u32[]{:S(2)}, u32[]{:S(2)}) %collective-permute-start.27) | collective-permute-done | bytes 524320 | tf_op jit(solution)/shard_map/ppermute | solution.py:33
  143.6 2.3 collective-permute-done.31
  154.0 2.4 slice-done.10
  156.4 2.6 fusion.42
  160.9 2.6 fusion.45
  165.1 3.1 collective-permute-done.15
  168.9 49.9 %collective-permute-done.16 = bf16[768,1536]{1,0:T(8,128)(2,1)S(1)} collective-permute-done((bf16[768,1536]{1,0:T(8,128)(2,1)S(1)}, bf16[768,1536]{1,0:T(8,128)(2,1)S(1)}, u32[]{:S(2)}, u32[]{:S(2)}) %collective-permute-start.16) | collective-permute-done | bytes 2359328 | tf_op jit(solution)/shard_map/ppermute | solution.py:17
  218.8 2.9 convert_add_fusion
  221.6 22.4 %collective-permute-done.40 = bf16[768,768]{1,0:T(8,128)(2,1)S(1)} collective-permute-done((bf16[768,768]{1,0:T(8,128)(2,1)S(1)}, bf16[768,768]{1,0:T(8,128)(2,1)S(1)}, u32[]{:S(2)}, u32[]{:S(2)}) %collective-permute-start.40) | collective-permute-done | bytes 1179680 | tf_op jit(solution)/shard_map/ppermute | solution.py:17
  246.2 22.8 %collective-permute-done.41 = bf16[768,768]{1,0:T(8,128)(2,1)S(1)} collective-permute-done((bf16[768,768]{1,0:T(8,128)(2,1)S(1)}, bf16[768,768]{1,0:T(8,128)(2,1)S(1)}, u32[]{:S(2)}, u32[]{:S(2)}) %collective-permute-start.41) | collective-permute-done | bytes 1179680 | tf_op jit(solution)/shard_map/ppermute | solution.py:17
  269.0 3.3 multiply_reduce_fusion
  273.3 5.1 %multiply_convert_fusion.3 = (bf16[768,768]{1,0:T(8,128)(2,1)}, bf16[768,768]{1,0:T(8,128)(2,1)}, bf16[768,768]{1,0:T(8,128)(2,1)S(1)}) fusion(f32[768,1536]{1,0:T(8,128)} %copy-done, bf16[768,768]{1,0:T(8,128)(2,1)} %copy-done.11, bf16[768,768]{1,0:T(8,128)(2,1)} %copy-done.10, f32[768]{0:T(1024)S(1)} %mul.109), kind=kLoop, calls=%fused_computation.54 | loop fusion | flops 11796480 | bytes 10619904 | tf_op jit(solution)/shard_map/convert.2
  278.3 5.1 %convolution_convert_fusion.8 = bf16[768,2048]{1,0:T(8,128)(2,1)S(1)} fusion(bf16[768,768]{1,0:T(8,128)(2,1)S(1)} %get-tuple-element.30, bf16[2,768,2048]{2,1,0:T(8,128)(2,1)} %param.10), kind=kOutput, calls=%fused_computation.30 | convolution fusion | flops 2417491968 | bytes 7471104 | tf_op jit(solution)/shard_map/dot_general | solution.py:11
  283.5 8.2 %fusion.72 = f32[16,128,2048]{2,1,0:T(8,128)} fusion(bf16[16,48,2048]{2,1,0:T(8,128)(2,1)S(1)} %bitcast.226, pred[2,16,48,128]{3,2,1,0:T(8,128)(4,1)S(1)} %compare_and_fusion), kind=kOutput, calls=%fused_computation.152 | convolution fusion | flops 402653184 | bytes 20021248 | tf_op jit(solution)/shard_map/gct,gcd->gtd/dot_general | solution.py:147
  291.7 4.5 multiply_convert_fusion.1
  296.2 6.3 %convolution_convert_fusion.6 = bf16[768,2048]{1,0:T(8,128)(2,1)} fusion(bf16[768,768]{1,0:T(8,128)(2,1)S(1)} %get-tuple-element.29, bf16[2,768,2048]{2,1,0:T(8,128)(2,1)} %param.10), kind=kOutput, calls=%fused_computation.28 | convolution fusion | flops 2417491968 | bytes 7471104 | tf_op jit(solution)/shard_map/dot_general | solution.py:11
  302.4 9.1 %add_convert_fusion.1 = bf16[16,128,2048]{2,1,0:T(8,128)(2,1)S(1)} fusion(f32[16,128,2048]{2,1,0:T(8,128)} %fusion.72, bf16[16,48,2048]{2,1,0:T(8,128)(2,1)} %bitcast.237, pred[2,16,48,128]{3,2,1,0:T(8,128)(4,1)S(1)} %compare_and_fusion), kind=kOutput, calls=%fused_computation.1 | convolution fusion | flops 411041792 | bytes 28409856 | tf_op jit(solution)/shard_map/gct,gcd->gtd/dot_general | solution.py:147
  311.6 2.6 slice.215
  314.2 2.3 copy-done.1
  316.5 8.5 %fusion.20 = bf16[768,2048]{1,0:T(8,128)(2,1)S(1)} fusion(bf16[2,2048,1536]{2,1,0:T(8,128)(2,1)} %param.9, bf16[768,768]{1,0:T(8,128)(2,1)S(1)} %copy-done.15, bf16[768,768]{1,0:T(8,128)(2,1)S(1)} %copy-done.14), kind=kOutput, calls=%fused_computation.32 | convolution fusion | flops 4838129664 | bytes 11796480 | tf_op jit(solution)/shard_map/dot_general | solution.py:11
  325.0 8.2 %fusion.71 = f32[16,128,2048]{2,1,0:T(8,128)} fusion(bf16[16,48,2048]{2,1,0:T(8,128)(2,1)S(1)} %bitcast.227, pred[2,16,48,128]{3,2,1,0:T(8,128)(4,1)S(1)} %compare_and_fusion), kind=kOutput, calls=%fused_computation.151 | convolution fusion | flops 402653184 | bytes 20021248 | tf_op jit(solution)/shard_map/gct,gcd->gtd/dot_general | solution.py:147
  333.2 6.4 %fusion.23 = bf16[768,2048]{1,0:T(8,128)(2,1)} fusion(bf16[2,2048,1536]{2,1,0:T(8,128)(2,1)S(1)} %bitcast.242, bf16[768,768]{1,0:T(8,128)(2,1)S(1)} %copy-done.19, bf16[768,768]{1,0:T(8,128)(2,1)S(1)} %copy-done.17), kind=kOutput, calls=%fused_computation.33 | convolution fusion | flops 4838129664 | bytes 11796480 | tf_op jit(solution)/shard_map/dot_general | solution.py:11
  339.6 9.1 %add_convert_fusion = bf16[16,128,2048]{2,1,0:T(8,128)(2,1)S(1)} fusion(f32[16,128,2048]{2,1,0:T(8,128)} %fusion.71, bf16[16,48,2048]{2,1,0:T(8,128)(2,1)} %bitcast.236, pred[2,16,48,128]{3,2,1,0:T(8,128)(4,1)S(1)} %compare_and_fusion), kind=kOutput, calls=%fused_computation | convolution fusion | flops 411041792 | bytes 28409856 | tf_op jit(solution)/shard_map/gct,gcd->gtd/dot_general | solution.py:147
  348.8 2.8 slice.232
  354.8 6.7 %fusion.33 = bf16[1,768,2048]{2,1,0:T(8,128)(2,1)} fusion(bf16[768,768]{1,0:T(8,128)(2,1)} %copy-done.21, bf16[768,2048]{1,0:T(8,128)(2,1)} %bitcast.235), kind=kOutput, calls=%fused_computation.41 | convolution fusion | flops 2417491968 | bytes 7471104 | tf_op jit(solution)/shard_map/dot_general | solution.py:11
  361.5 5.7 %fusion.1 = bf16[1,2048,1536]{2,1,0:T(8,128)(2,1)S(1)} fusion(bf16[768,2048]{1,0:T(8,128)(2,1)S(1)} %bitcast.231, bf16[768,768]{1,0:T(8,128)(2,1)S(1)} %copy-done.20, bf16[768,768]{1,0:T(8,128)(2,1)S(1)} %copy-done.18), kind=kOutput, calls=%fused_computation.6 | convolution fusion | flops 4839702528 | bytes 11796480 | tf_op jit(solution)/shard_map/dot_general | solution.py:11
  367.3 7.6 %fusion = bf16[1,2048,1536]{2,1,0:T(8,128)(2,1)} fusion(bf16[768,2048]{1,0:T(8,128)(2,1)S(1)} %bitcast.229, bf16[768,768]{1,0:T(8,128)(2,1)S(1)} %copy-done.16, bf16[768,768]{1,0:T(8,128)(2,1)S(1)} %copy-done.14), kind=kOutput, calls=%fused_computation.5 | convolution fusion | flops 4839702528 | bytes 11796480 | tf_op jit(solution)/shard_map/dot_general | solution.py:11
  378.3 9.0 %pad_maximum_fusion = bf16[2,2048,1536]{2,1,0:T(8,128)(2,1)} fusion(bf16[1,2048,1536]{2,1,0:T(8,128)(2,1)S(1)} %fusion.1, bf16[1,2048,1536]{2,1,0:T(8,128)(2,1)} %fusion), kind=kLoop, calls=%fused_computation.2 | loop fusion | flops 6291456 | bytes 25165824 | tf_op jit(solution)/shard_map/stack | solution.py:183
  393.8 4.0 fusion.32
  398.8 13.7 %collective-permute-done.46 = bf16[128,2048]{1,0:T(8,128)(2,1)S(1)} collective-permute-done((bf16[128,2048]{1,0:T(8,128)(2,1)S(1)}, bf16[128,2048]{1,0:T(8,128)(2,1)S(1)}, u32[]{:S(2)}, u32[]{:S(2)}) %collective-permute-start.46) | collective-permute-done | bytes 524320 | tf_op jit(solution)/shard_map/ppermute | solution.py:33
  417.7 11.0 %collective-permute-done.47 = bf16[128,2048]{1,0:T(8,128)(2,1)S(1)} collective-permute-done((bf16[128,2048]{1,0:T(8,128)(2,1)S(1)}, bf16[128,2048]{1,0:T(8,128)(2,1)S(1)}, u32[]{:S(2)}, u32[]{:S(2)}) %collective-permute-start.47) | collective-permute-done | bytes 524320 | tf_op jit(solution)/shard_map/ppermute | solution.py:33
  432.5 7.4 %collective-permute-done.23 = bf16[128,2048]{1,0:T(8,128)(2,1)S(1)} collective-permute-done((bf16[128,2048]{1,0:T(8,128)(2,1)S(1)}, bf16[128,2048]{1,0:T(8,128)(2,1)S(1)}, u32[]{:S(2)}, u32[]{:S(2)}) %collective-permute-start.23) | collective-permute-done | bytes 524320 | tf_op jit(solution)/shard_map/ppermute | solution.py:33
  439.9 2.5 fusion.57
  444.5 6.7 %collective-permute-done.48 = bf16[128,2048]{1,0:T(8,128)(2,1)S(1)} collective-permute-done((bf16[128,2048]{1,0:T(8,128)(2,1)S(1)}, bf16[128,2048]{1,0:T(8,128)(2,1)S(1)}, u32[]{:S(2)}, u32[]{:S(2)}) %collective-permute-start.48) | collective-permute-done | bytes 524320 | tf_op jit(solution)/shard_map/ppermute | solution.py:33
  451.2 2.7 fusion.51
  455.9 6.1 %pad_maximum_fusion.1 = bf16[2,768,2048]{2,1,0:T(8,128)(2,1)} fusion(bf16[1,768,2048]{2,1,0:T(8,128)(2,1)} %fusion.33, bf16[1,768,2048]{2,1,0:T(8,128)(2,1)} %fusion.32), kind=kLoop, calls=%fused_computation.7 | loop fusion | flops 3145728 | bytes 12582912 | tf_op jit(solution)/shard_map/stack | solution.py:186
  462.4 2.2 fusion.61
  464.6 7.5 %collective-permute-done.49 = bf16[128,2048]{1,0:T(8,128)(2,1)S(1)} collective-permute-done((bf16[128,2048]{1,0:T(8,128)(2,1)}, bf16[128,2048]{1,0:T(8,128)(2,1)S(1)}, u32[]{:S(2)}, u32[]{:S(2)}) %collective-permute-start.49) | collective-permute-done | bytes 524320 | tf_op jit(solution)/shard_map/ppermute | solution.py:33
  472.1 2.2 fusion.54
  (225 shorter events, 80.1 us)
Async XLA Ops:
  7.2 467.1 %reduce-scatter.2.cloned.1.call-start = ((), (), s32[]{:S(2)}) async-start(), calls=%async_computation.1 | async-start | bytes 69632 | tf_op jit(solution)/shard_map/reduce_scatter | solution.py:192
  7.2 32.5 %collective-permute-start = (bf16[128,2048]{1,0:T(8,128)(2,1)}, bf16[128,2048]{1,0:T(8,128)(2,1)S(1)}, u32[]{:S(2)}, u32[]{:S(2)}) collective-permute-start(bf16[128,2048]{1,0:T(8,128)(2,1)} %param.6), channel_id=1, source_target_pairs={{0,4},{1,5},{4,8},{5,9},{8,12},{9,13},{12,14},{13,15},{14,10},{15,... | collective-permute-start | bytes 1572872 | tf_op jit(solution)/shard_map/ppermute | solution.py:33
  10.3 29.6 %collective-permute-start.4 = (bf16[128,2048]{1,0:T(8,128)(2,1)}, bf16[128,2048]{1,0:T(8,128)(2,1)S(1)}, u32[]{:S(2)}, u32[]{:S(2)}) collective-permute-start(bf16[128,2048]{1,0:T(8,128)(2,1)} %param.6), channel_id=1, source_target_pairs={{0,2},{1,3},{4,0},{5,1},{8,4},{9,5},{12,8},{13,9},{14,12},{15,13},... | collective-permute-start | bytes 1572872 | tf_op jit(solution)/shard_map/ppermute | solution.py:33
  10.3 72.8 %collective-permute-start.7 = (bf16[128,2048]{1,0:T(8,128)(2,1)}, bf16[128,2048]{1,0:T(8,128)(2,1)S(1)}, u32[]{:S(2)}, u32[]{:S(2)}) collective-permute-start(bf16[128,2048]{1,0:T(8,128)(2,1)} %param.6), channel_id=1, source_target_pairs={{0,1},{1,0},{2,3},{3,2},{4,5},{5,4},{6,7},{7,6},{8,9},{9,8},{10,11... | collective-permute-start | bytes 1572872 | tf_op jit(solution)/shard_map/ppermute | solution.py:38
  10.3 135.8 %collective-permute-start.32 = (bf16[128,2048]{1,0:T(8,128)(2,1)}, bf16[128,2048]{1,0:T(8,128)(2,1)S(1)}, u32[]{:S(2)}, u32[]{:S(2)}) collective-permute-start(bf16[128,2048]{1,0:T(8,128)(2,1)} %param.11), channel_id=1, source_target_pairs={{0,1},{1,0},{2,3},{3,2},{4,5},{5,4},{6,7},{7,6},{8,9},{9,8},{10,11... | collective-permute-start | bytes 1572872 | tf_op jit(solution)/shard_map/ppermute | solution.py:38
  39.7 14.2 %collective-permute-start.1 = (bf16[128,2048]{1,0:T(8,128)(2,1)S(1)}, bf16[128,2048]{1,0:T(8,128)(2,1)S(1)}, u32[]{:S(2)}, u32[]{:S(2)}) collective-permute-start(bf16[128,2048]{1,0:T(8,128)(2,1)S(1)} %collective-permute-done), channel_id=1, source_target_pairs={{0,4},{1,5},{4,8},{5,9},{8,12},{9,13},{12,14},{13,15},{14,10},{15,... | collective-permute-start | bytes 1572872 | tf_op jit(solution)/shard_map/ppermute | solution.py:33
  39.9 14.4 %collective-permute-start.5 = (bf16[128,2048]{1,0:T(8,128)(2,1)S(1)}, bf16[128,2048]{1,0:T(8,128)(2,1)S(1)}, u32[]{:S(2)}, u32[]{:S(2)}) collective-permute-start(bf16[128,2048]{1,0:T(8,128)(2,1)S(1)} %collective-permute-done.4), channel_id=1, source_target_pairs={{0,2},{1,3},{4,0},{5,1},{8,4},{9,5},{12,8},{13,9},{14,12},{15,13},... | collective-permute-start | bytes 1572872 | tf_op jit(solution)/shard_map/ppermute | solution.py:33
  53.9 13.4 %collective-permute-start.2 = (bf16[128,2048]{1,0:T(8,128)(2,1)S(1)}, bf16[128,2048]{1,0:T(8,128)(2,1)S(1)}, u32[]{:S(2)}, u32[]{:S(2)}) collective-permute-start(bf16[128,2048]{1,0:T(8,128)(2,1)S(1)} %collective-permute-done.1), channel_id=1, source_target_pairs={{0,4},{1,5},{4,8},{5,9},{8,12},{9,13},{12,14},{13,15},{14,10},{15,... | collective-permute-start | bytes 1572872 | tf_op jit(solution)/shard_map/ppermute | solution.py:33
  54.3 29.9 %collective-permute-start.8 = (bf16[128,2048]{1,0:T(8,128)(2,1)S(1)}, bf16[128,2048]{1,0:T(8,128)(2,1)S(1)}, u32[]{:S(2)}, u32[]{:S(2)}) collective-permute-start(bf16[128,2048]{1,0:T(8,128)(2,1)S(1)} %collective-permute-done), channel_id=1, source_target_pairs={{0,1},{1,0},{2,3},{3,2},{4,5},{5,4},{6,7},{7,6},{8,9},{9,8},{10,11... | collective-permute-start | bytes 1572872 | tf_op jit(solution)/shard_map/ppermute | solution.py:38
  54.3 14.4 %collective-permute-start.6 = (bf16[128,2048]{1,0:T(8,128)(2,1)S(1)}, bf16[128,2048]{1,0:T(8,128)(2,1)S(1)}, u32[]{:S(2)}, u32[]{:S(2)}) collective-permute-start(bf16[128,2048]{1,0:T(8,128)(2,1)S(1)} %collective-permute-done.5), channel_id=1, source_target_pairs={{0,2},{1,3},{4,0},{5,1},{8,4},{9,5},{12,8},{13,9},{14,12},{15,13},... | collective-permute-start | bytes 1572872 | tf_op jit(solution)/shard_map/ppermute | solution.py:33
  67.3 12.5 %collective-permute-start.3 = (bf16[128,2048]{1,0:T(8,128)(2,1)S(1)}, bf16[128,2048]{1,0:T(8,128)(2,1)S(1)}, u32[]{:S(2)}, u32[]{:S(2)}) collective-permute-start(bf16[128,2048]{1,0:T(8,128)(2,1)S(1)} %collective-permute-done.2), channel_id=1, source_target_pairs={{0,4},{1,5},{4,8},{5,9},{8,12},{9,13},{12,14},{13,15},{14,10},{15,... | collective-permute-start | bytes 1572872 | tf_op jit(solution)/shard_map/ppermute | solution.py:33
  68.8 30.6 %collective-permute-start.14 = (bf16[128,2048]{1,0:T(8,128)(2,1)S(1)}, bf16[128,2048]{1,0:T(8,128)(2,1)S(1)}, u32[]{:S(2)}, u32[]{:S(2)}) collective-permute-start(bf16[128,2048]{1,0:T(8,128)(2,1)S(1)} %collective-permute-done.4), channel_id=1, source_target_pairs={{0,1},{1,0},{2,3},{3,2},{4,5},{5,4},{6,7},{7,6},{8,9},{9,8},{10,11... | collective-permute-start | bytes 1572872 | tf_op jit(solution)/shard_map/ppermute | solution.py:38
  79.8 5.5 %collective-permute-start.9 = (bf16[128,2048]{1,0:T(8,128)(2,1)S(1)}, bf16[128,2048]{1,0:T(8,128)(2,1)S(1)}, u32[]{:S(2)}, u32[]{:S(2)}) collective-permute-start(bf16[128,2048]{1,0:T(8,128)(2,1)S(1)} %collective-permute-done.1), channel_id=1, source_target_pairs={{0,1},{1,0},{2,3},{3,2},{4,5},{5,4},{6,7},{7,6},{8,9},{9,8},{10,11... | collective-permute-start | bytes 1572872 | tf_op jit(solution)/shard_map/ppermute | solution.py:38
  83.1 14.3 %collective-permute-start.28 = (bf16[128,2048]{1,0:T(8,128)(2,1)S(1)}, bf16[128,2048]{1,0:T(8,128)(2,1)S(1)}, u32[]{:S(2)}, u32[]{:S(2)}) collective-permute-start(bf16[128,2048]{1,0:T(8,128)(2,1)S(1)} %copy-done.22), channel_id=1, source_target_pairs={{0,2},{1,3},{4,0},{5,1},{8,4},{9,5},{12,8},{13,9},{14,12},{15,13},... | collective-permute-start | bytes 1572872 | tf_op jit(solution)/shard_map/ppermute | solution.py:33
  84.2 2.2 collective-permute-start.10
  85.3 2.2 collective-permute-start.11
  86.4 2.2 collective-permute-start.12
  87.5 11.1 %collective-permute-start.13 = (bf16[128,2048]{1,0:T(8,128)(2,1)S(1)}, bf16[128,2048]{1,0:T(8,128)(2,1)S(1)}, u32[]{:S(2)}, u32[]{:S(2)}) collective-permute-start(bf16[128,2048]{1,0:T(8,128)(2,1)S(1)} %collective-permute-done.5), channel_id=1, source_target_pairs={{0,1},{1,0},{2,3},{3,2},{4,5},{5,4},{6,7},{7,6},{8,9},{9,8},{10,11... | collective-permute-start | bytes 1572872 | tf_op jit(solution)/shard_map/ppermute | solution.py:38
  88.6 27.1 %collective-permute-start.25 = (bf16[128,2048]{1,0:T(8,128)(2,1)S(1)}, bf16[128,2048]{1,0:T(8,128)(2,1)S(1)}, u32[]{:S(2)}, u32[]{:S(2)}) collective-permute-start(bf16[128,2048]{1,0:T(8,128)(2,1)S(1)} %copy-done.22), channel_id=1, source_target_pairs={{0,4},{1,5},{4,8},{5,9},{8,12},{9,13},{12,14},{13,15},{14,10},{15,... | collective-permute-start | bytes 1572872 | tf_op jit(solution)/shard_map/ppermute | solution.py:33
  97.4 21.3 %collective-permute-start.29 = (bf16[128,2048]{1,0:T(8,128)(2,1)S(1)}, bf16[128,2048]{1,0:T(8,128)(2,1)S(1)}, u32[]{:S(2)}, u32[]{:S(2)}) collective-permute-start(bf16[128,2048]{1,0:T(8,128)(2,1)S(1)} %collective-permute-done.28), channel_id=1, source_target_pairs={{0,2},{1,3},{4,0},{5,1},{8,4},{9,5},{12,8},{13,9},{14,12},{15,13},... | collective-permute-start | bytes 1572872 | tf_op jit(solution)/shard_map/ppermute | solution.py:33
  98.5 53.9 %collective-permute-start.39 = (bf16[128,2048]{1,0:T(8,128)(2,1)S(1)}, bf16[128,2048]{1,0:T(8,128)(2,1)S(1)}, u32[]{:S(2)}, u32[]{:S(2)}) collective-permute-start(bf16[128,2048]{1,0:T(8,128)(2,1)S(1)} %collective-permute-done.28), channel_id=1, source_target_pairs={{0,1},{1,0},{2,3},{3,2},{4,5},{5,4},{6,7},{7,6},{8,9},{9,8},{10,11... | collective-permute-start | bytes 1572872 | tf_op jit(solution)/shard_map/ppermute | solution.py:38
  114.1 54.1 %collective-permute-start.15 = (bf16[768,1536]{1,0:T(8,128)(2,1)S(1)}, bf16[768,1536]{1,0:T(8,128)(2,1)S(1)}, u32[]{:S(2)}, u32[]{:S(2)}) collective-permute-start(bf16[768,1536]{1,0:T(8,128)(2,1)S(1)} %fusion.14), channel_id=1, source_target_pairs={{0,16},{16,0},{1,17},{17,1},{2,18},{18,2},{3,19},{19,3},{4,20},{20... | collective-permute-start | bytes 7077896 | tf_op jit(solution)/shard_map/ppermute | solution.py:17
  115.7 14.1 %collective-permute-start.26 = (bf16[128,2048]{1,0:T(8,128)(2,1)S(1)}, bf16[128,2048]{1,0:T(8,128)(2,1)S(1)}, u32[]{:S(2)}, u32[]{:S(2)}) collective-permute-start(bf16[128,2048]{1,0:T(8,128)(2,1)S(1)} %collective-permute-done.25), channel_id=1, source_target_pairs={{0,4},{1,5},{4,8},{5,9},{8,12},{9,13},{12,14},{13,15},{14,10},{15,... | collective-permute-start | bytes 1572872 | tf_op jit(solution)/shard_map/ppermute | solution.py:33
  118.7 13.8 %collective-permute-start.30 = (bf16[128,2048]{1,0:T(8,128)(2,1)S(1)}, bf16[128,2048]{1,0:T(8,128)(2,1)S(1)}, u32[]{:S(2)}, u32[]{:S(2)}) collective-permute-start(bf16[128,2048]{1,0:T(8,128)(2,1)S(1)} %collective-permute-done.29), channel_id=1, source_target_pairs={{0,2},{1,3},{4,0},{5,1},{8,4},{9,5},{12,8},{13,9},{14,12},{15,13},... | collective-permute-start | bytes 1572872 | tf_op jit(solution)/shard_map/ppermute | solution.py:33
  129.8 13.2 %collective-permute-start.27 = (bf16[128,2048]{1,0:T(8,128)(2,1)S(1)}, bf16[128,2048]{1,0:T(8,128)(2,1)S(1)}, u32[]{:S(2)}, u32[]{:S(2)}) collective-permute-start(bf16[128,2048]{1,0:T(8,128)(2,1)S(1)} %collective-permute-done.26), channel_id=1, source_target_pairs={{0,4},{1,5},{4,8},{5,9},{8,12},{9,13},{12,14},{13,15},{14,10},{15,... | collective-permute-start | bytes 1572872 | tf_op jit(solution)/shard_map/ppermute | solution.py:33
  132.5 13.4 %collective-permute-start.31 = (bf16[128,2048]{1,0:T(8,128)(2,1)S(1)}, bf16[128,2048]{1,0:T(8,128)(2,1)S(1)}, u32[]{:S(2)}, u32[]{:S(2)}) collective-permute-start(bf16[128,2048]{1,0:T(8,128)(2,1)S(1)} %collective-permute-done.30), channel_id=1, source_target_pairs={{0,2},{1,3},{4,0},{5,1},{8,4},{9,5},{12,8},{13,9},{14,12},{15,13},... | collective-permute-start | bytes 1572872 | tf_op jit(solution)/shard_map/ppermute | solution.py:33
  143.0 75.8 %collective-permute-start.16 = (bf16[768,1536]{1,0:T(8,128)(2,1)S(1)}, bf16[768,1536]{1,0:T(8,128)(2,1)S(1)}, u32[]{:S(2)}, u32[]{:S(2)}) collective-permute-start(bf16[768,1536]{1,0:T(8,128)(2,1)S(1)} %fusion.17), channel_id=1, source_target_pairs={{0,16},{16,0},{1,17},{17,1},{2,18},{18,2},{3,19},{19,3},{4,20},{20... | collective-permute-start | bytes 7077896 | tf_op jit(solution)/shard_map/ppermute | solution.py:17
  146.1 2.5 collective-permute-start.34
  149.7 1.9 collective-permute-start.37
  150.5 1.9 collective-permute-start.38
  159.0 85.0 %collective-permute-start.40 = (bf16[768,768]{1,0:T(8,128)(2,1)S(1)}, bf16[768,768]{1,0:T(8,128)(2,1)S(1)}, u32[]{:S(2)}, u32[]{:S(2)}) collective-permute-start(bf16[768,768]{1,0:T(8,128)(2,1)S(1)} %fusion.42), channel_id=1, source_target_pairs={{0,16},{16,0},{1,17},{17,1},{2,18},{18,2},{3,19},{19,3},{4,20},{20... | collective-permute-start | bytes 3538952 | tf_op jit(solution)/shard_map/ppermute | solution.py:17
  163.5 105.4 %collective-permute-start.41 = (bf16[768,768]{1,0:T(8,128)(2,1)S(1)}, bf16[768,768]{1,0:T(8,128)(2,1)S(1)}, u32[]{:S(2)}, u32[]{:S(2)}) collective-permute-start(bf16[768,768]{1,0:T(8,128)(2,1)S(1)} %fusion.45), channel_id=1, source_target_pairs={{0,16},{16,0},{1,17},{17,1},{2,18},{18,2},{3,19},{19,3},{4,20},{20... | collective-permute-start | bytes 3538952 | tf_op jit(solution)/shard_map/ppermute | solution.py:17
  316.5 58.4 %collective-permute-start.17 = (bf16[8,128,2048]{2,1,0:T(8,128)(2,1)}, bf16[8,128,2048]{2,1,0:T(8,128)(2,1)}, u32[]{:S(2)}, u32[]{:S(2)}) collective-permute-start(bf16[8,128,2048]{2,1,0:T(8,128)(2,1)} %slice.215), channel_id=1, source_target_pairs={{0,1},{1,0},{2,3},{3,2},{4,5},{5,4},{6,7},{7,6},{8,9},{9,8},{10,11... | collective-permute-start | bytes 12582920 | tf_op jit(solution)/shard_map/ppermute | solution.py:38
  353.3 34.2 %collective-permute-start.42 = (bf16[8,128,2048]{2,1,0:T(8,128)(2,1)}, bf16[8,128,2048]{2,1,0:T(8,128)(2,1)}, u32[]{:S(2)}, u32[]{:S(2)}) collective-permute-start(bf16[8,128,2048]{2,1,0:T(8,128)(2,1)} %slice.232), channel_id=1, source_target_pairs={{0,1},{1,0},{2,3},{3,2},{4,5},{5,4},{6,7},{7,6},{8,9},{9,8},{10,11... | collective-permute-start | bytes 12582920 | tf_op jit(solution)/shard_map/ppermute | solution.py:38
  376.5 14.1 %collective-permute-start.18 = (bf16[128,2048]{1,0:T(8,128)(2,1)S(1)}, bf16[128,2048]{1,0:T(8,128)(2,1)S(1)}, u32[]{:S(2)}, u32[]{:S(2)}) collective-permute-start(bf16[128,2048]{1,0:T(8,128)(2,1)S(1)} %get-tuple-element.23), channel_id=1, source_target_pairs={{0,4},{1,5},{4,8},{5,9},{8,12},{9,13},{12,14},{13,15},{14,10},{15,... | collective-permute-start | bytes 1572872 | tf_op jit(solution)/shard_map/ppermute | solution.py:33
  387.2 26.6 %collective-permute-start.22 = (bf16[128,2048]{1,0:T(8,128)(2,1)S(1)}, bf16[128,2048]{1,0:T(8,128)(2,1)S(1)}, u32[]{:S(2)}, u32[]{:S(2)}) collective-permute-start(bf16[128,2048]{1,0:T(8,128)(2,1)S(1)} %get-tuple-element.24), channel_id=1, source_target_pairs={{0,2},{1,3},{4,0},{5,1},{8,4},{9,5},{12,8},{13,9},{14,12},{15,13},... | collective-permute-start | bytes 1572872 | tf_op jit(solution)/shard_map/ppermute | solution.py:33
  389.2 23.3 %collective-permute-start.46 = (bf16[128,2048]{1,0:T(8,128)(2,1)S(1)}, bf16[128,2048]{1,0:T(8,128)(2,1)S(1)}, u32[]{:S(2)}, u32[]{:S(2)}) collective-permute-start(bf16[128,2048]{1,0:T(8,128)(2,1)S(1)} %get-tuple-element.18), channel_id=1, source_target_pairs={{0,2},{1,3},{4,0},{5,1},{8,4},{9,5},{12,8},{13,9},{14,12},{15,13},... | collective-permute-start | bytes 1572872 | tf_op jit(solution)/shard_map/ppermute | solution.py:33
  391.9 22.0 %collective-permute-start.19 = (bf16[128,2048]{1,0:T(8,128)(2,1)S(1)}, bf16[128,2048]{1,0:T(8,128)(2,1)S(1)}, u32[]{:S(2)}, u32[]{:S(2)}) collective-permute-start(bf16[128,2048]{1,0:T(8,128)(2,1)S(1)} %fusion.59), channel_id=1, source_target_pairs={{0,4},{1,5},{4,8},{5,9},{8,12},{9,13},{12,14},{13,15},{14,10},{15,... | collective-permute-start | bytes 1572872 | tf_op jit(solution)/shard_map/ppermute | solution.py:33
  397.8 19.9 %collective-permute-start.43 = (bf16[128,2048]{1,0:T(8,128)(2,1)S(1)}, bf16[128,2048]{1,0:T(8,128)(2,1)S(1)}, u32[]{:S(2)}, u32[]{:S(2)}) collective-permute-start(bf16[128,2048]{1,0:T(8,128)(2,1)S(1)} %get-tuple-element.17), channel_id=1, source_target_pairs={{0,4},{1,5},{4,8},{5,9},{8,12},{9,13},{12,14},{13,15},{14,10},{15,... | collective-permute-start | bytes 1572872 | tf_op jit(solution)/shard_map/ppermute | solution.py:33
  413.8 14.9 %collective-permute-start.47 = (bf16[128,2048]{1,0:T(8,128)(2,1)S(1)}, bf16[128,2048]{1,0:T(8,128)(2,1)S(1)}, u32[]{:S(2)}, u32[]{:S(2)}) collective-permute-start(bf16[128,2048]{1,0:T(8,128)(2,1)S(1)} %fusion.50), channel_id=1, source_target_pairs={{0,2},{1,3},{4,0},{5,1},{8,4},{9,5},{12,8},{13,9},{14,12},{15,13},... | collective-permute-start | bytes 1572872 | tf_op jit(solution)/shard_map/ppermute | solution.py:33
  415.6 16.9 %collective-permute-start.20 = (bf16[128,2048]{1,0:T(8,128)(2,1)S(1)}, bf16[128,2048]{1,0:T(8,128)(2,1)S(1)}, u32[]{:S(2)}, u32[]{:S(2)}) collective-permute-start(bf16[128,2048]{1,0:T(8,128)(2,1)S(1)} %get-tuple-element.21), channel_id=1, source_target_pairs={{0,4},{1,5},{4,8},{5,9},{8,12},{9,13},{12,14},{13,15},{14,10},{15,... | collective-permute-start | bytes 1572872 | tf_op jit(solution)/shard_map/ppermute | solution.py:33
  417.6 22.3 %collective-permute-start.23 = (bf16[128,2048]{1,0:T(8,128)(2,1)S(1)}, bf16[128,2048]{1,0:T(8,128)(2,1)S(1)}, u32[]{:S(2)}, u32[]{:S(2)}) collective-permute-start(bf16[128,2048]{1,0:T(8,128)(2,1)S(1)} %get-tuple-element.22), channel_id=1, source_target_pairs={{0,2},{1,3},{4,0},{5,1},{8,4},{9,5},{12,8},{13,9},{14,12},{15,13},... | collective-permute-start | bytes 1572872 | tf_op jit(solution)/shard_map/ppermute | solution.py:33
  430.4 14.1 %collective-permute-start.44 = (bf16[128,2048]{1,0:T(8,128)(2,1)S(1)}, bf16[128,2048]{1,0:T(8,128)(2,1)S(1)}, u32[]{:S(2)}, u32[]{:S(2)}) collective-permute-start(bf16[128,2048]{1,0:T(8,128)(2,1)S(1)} %get-tuple-element.15), channel_id=1, source_target_pairs={{0,4},{1,5},{4,8},{5,9},{8,12},{9,13},{12,14},{13,15},{14,10},{15,... | collective-permute-start | bytes 1572872 | tf_op jit(solution)/shard_map/ppermute | solution.py:33
  432.2 18.9 %collective-permute-start.48 = (bf16[128,2048]{1,0:T(8,128)(2,1)S(1)}, bf16[128,2048]{1,0:T(8,128)(2,1)S(1)}, u32[]{:S(2)}, u32[]{:S(2)}) collective-permute-start(bf16[128,2048]{1,0:T(8,128)(2,1)S(1)} %get-tuple-element.16), channel_id=1, source_target_pairs={{0,2},{1,3},{4,0},{5,1},{8,4},{9,5},{12,8},{13,9},{14,12},{15,13},... | collective-permute-start | bytes 1572872 | tf_op jit(solution)/shard_map/ppermute | solution.py:33
  442.4 20.0 %collective-permute-start.24 = (bf16[128,2048]{1,0:T(8,128)(2,1)}, bf16[128,2048]{1,0:T(8,128)(2,1)S(1)}, u32[]{:S(2)}, u32[]{:S(2)}) collective-permute-start(bf16[128,2048]{1,0:T(8,128)(2,1)} %get-tuple-element.20), channel_id=1, source_target_pairs={{0,2},{1,3},{4,0},{5,1},{8,4},{9,5},{12,8},{13,9},{14,12},{15,13},... | collective-permute-start | bytes 1572872 | tf_op jit(solution)/shard_map/ppermute | solution.py:33
  442.5 20.0 %collective-permute-start.21 = (bf16[128,2048]{1,0:T(8,128)(2,1)S(1)}, bf16[128,2048]{1,0:T(8,128)(2,1)S(1)}, u32[]{:S(2)}, u32[]{:S(2)}) collective-permute-start(bf16[128,2048]{1,0:T(8,128)(2,1)S(1)} %get-tuple-element.19), channel_id=1, source_target_pairs={{0,4},{1,5},{4,8},{5,9},{8,12},{9,13},{12,14},{13,15},{14,10},{15,... | collective-permute-start | bytes 1572872 | tf_op jit(solution)/shard_map/ppermute | solution.py:33
  453.9 18.2 %collective-permute-start.49 = (bf16[128,2048]{1,0:T(8,128)(2,1)}, bf16[128,2048]{1,0:T(8,128)(2,1)S(1)}, u32[]{:S(2)}, u32[]{:S(2)}) collective-permute-start(bf16[128,2048]{1,0:T(8,128)(2,1)} %get-tuple-element.14), channel_id=1, source_target_pairs={{0,2},{1,3},{4,0},{5,1},{8,4},{9,5},{12,8},{13,9},{14,12},{15,13},... | collective-permute-start | bytes 1572872 | tf_op jit(solution)/shard_map/ppermute | solution.py:33
  453.9 18.2 %collective-permute-start.45 = (bf16[128,2048]{1,0:T(8,128)(2,1)}, bf16[128,2048]{1,0:T(8,128)(2,1)S(1)}, u32[]{:S(2)}, u32[]{:S(2)}) collective-permute-start(bf16[128,2048]{1,0:T(8,128)(2,1)} %get-tuple-element.13), channel_id=1, source_target_pairs={{0,4},{1,5},{4,8},{5,9},{8,12},{9,13},{12,14},{13,15},{14,10},{15,... | collective-permute-start | bytes 1572872 | tf_op jit(solution)/shard_map/ppermute | solution.py:33
  (37 other events, 444.9 us)
Sparse Core Ops, SparseCore 0:
  354.9 51.5 reduce-scatter.1

commit v3 on v2

--- a/solution.py
+++ b/solution.py
@@ -142,7 +142,7 @@
             .reshape(rows, width)
         )
 
-    def combine(values, more):
+    def total_of(values):
         total = sum(
             jnp.einsum(
                 "gct,gcd->gtd",
@@ -152,21 +152,29 @@
             )
             for l in range(local_count)
         )
-        return scatter_ring(total.astype(BF16), more)
+        return total.astype(BF16)
 
     each = range(local_count)
     x_slots = [slots(x_all, l) for l in each]
     og_slots = [slots(og_all, l) for l in each]
     preact = [dp_sum(dot(x_slots[l], gate_up_weight[l], ((1,), (0,))).astype(BF16)) for l in each]
-    raw_grad = [dp_sum(dot(og_slots[l], down_weight[l], ((1,), (1,))).astype(BF16)) for l in each]
-    hidden_w, preact_grad, route_part = [], [], []
+    hidden_w = []
+    for l in each:
+        gate, up = preact[l][:, :units], preact[l][:, units:]
+        w = slot_weight[l].reshape(rows, 1)
+        hidden_w.append((w * (gate * jax.nn.sigmoid(gate) * up)).astype(BF16))
+    layer_total = total_of([dot(hidden_w[l], down_weight[l], ((1,), (0,))).astype(BF16) for l in each])
+    grad_parts = [dot(og_slots[l], down_weight[l], ((1,), (1,))).astype(BF16) for l in each]
+    grad_parts[-1], layer_total = lax.optimization_barrier((grad_parts[-1], layer_total))
+    raw_grad = [dp_sum(part) for part in grad_parts]
+    layer_out = scatter_ring(layer_total, True)
+    preact_grad, route_part = [], []
     for l in each:
         w = slot_weight[l].reshape(rows, 1)
         gate, up = preact[l][:, :units], preact[l][:, units:]
         sig = jax.nn.sigmoid(gate)
         act = gate * sig
         hidden = act * up
-        hidden_w.append((w * hidden).astype(BF16))
         route_part.append(jnp.sum(hidden * raw_grad[l], axis=1).reshape(groups, capacity))
         grad = w * raw_grad[l]
         preact_grad.append(
@@ -174,11 +182,9 @@
                 [grad * up * sig * (1.0 + gate * (1.0 - sig)), grad * act], axis=1
             ).astype(BF16)
         )
-    layer_out = combine(
-        [dot(hidden_w[l], down_weight[l], ((1,), (0,))).astype(BF16) for l in each], True
-    )
-    token_grad = combine(
-        [dot(preact_grad[l], gate_up_weight[l], ((1,), (1,))).astype(BF16) for l in each], False
+    token_grad = scatter_ring(
+        total_of([dot(preact_grad[l], gate_up_weight[l], ((1,), (1,))).astype(BF16) for l in each]),
+        False,
     )
     gate_up_grad = jnp.stack(
         [dot(x_slots[l], preact_grad[l], ((0,), (0,))).astype(BF16) for l in each]

time: 490 us -> 455 us (0.929)
  waiting for transfers between devices: 205 us -> 183 us
  other arithmetic: 55.3 us -> 43.1 us
  local copies, waits for them, and re-layouts: 29.7 us -> 35.5 us
    ppermute x4, waiting for transfers between devices: 98.1 us -> 76.5 us  [dp_sum(): other = lax.ppermute(part, 'dp', [(0, 1), (1, 0)])]
    unnamed x98 -> x104, local copies, waits for them, and re-layouts: 23.1 us -> 28.8 us
  transfers between devices with their start and end apart: 51 -> 51, of which waited for: 25 -> 29; matrix products, arithmetic and copies ran while one was open for 31% -> 35% of each run, Pallas kernels for 0% -> 0%
where the time goes in v3:
time: 455 us; the launch traced here: 447 us
  waiting for transfers between devices  183 us (40%)
  matrix products  113 us (25%)
  other arithmetic  43.1 us (9%)
  local copies, waits for them, and re-layouts  35.5 us (8%)
  starting transfers between devices  34.8 us (8%)
  blocking collectives  22.4 us (5%)
  between operations  15.3 us (3%)
    ppermute x28, waiting for transfers between devices, move(): lax.ppermute(array, 'expert', ring_step(lax.axis_size('expert'), step))  102 us
    ppermute x4, waiting for transfers between devices, dp_sum(): other = lax.ppermute(part, 'dp', [(0, 1), (1, 0)])  76.5 us
    dot_general x12, matrix products, dot(): lax.dot_general(a, b, (contract, ((), ())), preferred_element_type=F32)  69.6 us
    dot_general x4, matrix products, total_of(): jnp.einsum('gct,gcd->gtd', pick[l], values[l].reshape(groups, capacity, w...  34.6 us
    unnamed x104, local copies, waits for them, and re-layouts  28.8 us
    ppermute x28, starting transfers between devices, move(): lax.ppermute(array, 'expert', ring_step(lax.axis_size('expert'), step))  27.9 us
    all_gather x1, blocking collectives, local(): lax.all_gather(jnp.concatenate([expert_ids.astype(F32), route_weights], a...  22.4 us
    convert_element_type x7, other arithmetic, scatter_ring(): first = move(first.astype(BF16), 1).astype(F32)  15.6 us
  transfers between devices with their start and end apart: 51, of which 29 were waited for; matrix products, arithmetic and copies ran while one was open for 35% of the time, Pallas kernels for 0%

profile of v3, /device:TPU:0, one launch (start us, length us, event | category | flops | bytes accessed | tf_op | source)
XLA Modules:
  0.0 447.0 jit_solution(2488346349250852840)
XLA Ops:
  7.2 3.1 collective-permute-start
  16.0 22.4 %all_gather.3 = f32[2048,16]{0,1:T(8,128)S(1)} all-gather(f32[128,16]{0,1:T(8,128)S(1)} %pad_maximum_fusion.9), channel_id=1, replica_groups=mesh['dp'=2,'expert'=16] {'expert'}, dimensions={0}, use_global_device_ids=true | all-gather | bytes 139264 | tf_op jit(solution)/shard_map/all_gather | solution.py:115
  42.3 12.0 %collective-permute-done.1 = bf16[128,2048]{1,0:T(8,128)(2,1)} collective-permute-done((bf16[128,2048]{1,0:T(8,128)(2,1)S(1)}, bf16[128,2048]{1,0:T(8,128)(2,1)}, u32[]{:S(2)}, u32[]{:S(2)}) %collective-permute-start.1) | collective-permute-done | bytes 524320 | tf_op jit(solution)/shard_map/ppermute | solution.py:33
  58.1 9.9 %collective-permute-done.2 = bf16[128,2048]{1,0:T(8,128)(2,1)} collective-permute-done((bf16[128,2048]{1,0:T(8,128)(2,1)}, bf16[128,2048]{1,0:T(8,128)(2,1)}, u32[]{:S(2)}, u32[]{:S(2)}) %collective-permute-start.2) | collective-permute-done | bytes 524320 | tf_op jit(solution)/shard_map/ppermute | solution.py:33
  72.4 8.3 %collective-permute-done.3 = bf16[128,2048]{1,0:T(8,128)(2,1)S(1)} collective-permute-done((bf16[128,2048]{1,0:T(8,128)(2,1)}, bf16[128,2048]{1,0:T(8,128)(2,1)S(1)}, u32[]{:S(2)}, u32[]{:S(2)}) %collective-permute-start.3) | collective-permute-done | bytes 524320 | tf_op jit(solution)/shard_map/ppermute | solution.py:33
  90.4 9.1 %collective-permute-done.10 = bf16[128,2048]{1,0:T(8,128)(2,1)S(1)} collective-permute-done((bf16[128,2048]{1,0:T(8,128)(2,1)S(1)}, bf16[128,2048]{1,0:T(8,128)(2,1)S(1)}, u32[]{:S(2)}, u32[]{:S(2)}) %collective-permute-start.10) | collective-permute-done | bytes 524320 | tf_op jit(solution)/shard_map/ppermute | solution.py:33
  103.9 4.6 %convolution_convert_fusion.8 = bf16[16,48,2048]{2,1,0:T(8,128)(2,1)S(1)} fusion(bf16[16,128,2048]{2,1,0:T(8,128)(2,1)} %bitcast_dynamic-update-slice_fusion, pred[2,16,48,128]{3,2,1,0:T(8,128)(4,1)S(1)} %compare_and_fusion), kind=kOutput, calls=%fused_computation.30 | convolution fusion | flops 404226048 | bytes 11632640 | tf_op jit(solution)/shard_map/gct,gtd->gcd/dot_general | solution.py:140
  108.6 9.2 %fusion.14 = bf16[768,1536]{1,0:T(8,128)(2,1)S(1)} fusion(bf16[768,2048]{1,0:T(8,128)(2,1)S(1)} %bitcast.230, bf16[2,2048,1536]{2,1,0:T(8,128)(2,1)} %param.9), kind=kOutput, calls=%fused_computation.22 | convolution fusion | flops 4833017856 | bytes 11796480 | tf_op jit(solution)/shard_map/dot_general | solution.py:11
  122.8 8.2 %fusion.17 = bf16[768,1536]{1,0:T(8,128)(2,1)S(1)} fusion(bf16[768,2048]{1,0:T(8,128)(2,1)S(1)} %bitcast.228, bf16[2,2048,1536]{2,1,0:T(8,128)(2,1)} %param.9), kind=kOutput, calls=%fused_computation.23 | convolution fusion | flops 4833017856 | bytes 11796480 | tf_op jit(solution)/shard_map/dot_general | solution.py:11
  131.0 2.5 collective-permute-done.5
  137.0 9.7 %collective-permute-done.6 = bf16[128,2048]{1,0:T(8,128)(2,1)S(1)} collective-permute-done((bf16[128,2048]{1,0:T(8,128)(2,1)S(1)}, bf16[128,2048]{1,0:T(8,128)(2,1)S(1)}, u32[]{:S(2)}, u32[]{:S(2)}) %collective-permute-start.6) | collective-permute-done | bytes 524320 | tf_op jit(solution)/shard_map/ppermute | solution.py:33
  159.4 2.6 fusion.45
  163.8 3.7 fusion.42
  167.5 55.0 %collective-permute-done.31 = bf16[768,1536]{1,0:T(8,128)(2,1)S(1)} collective-permute-done((bf16[768,1536]{1,0:T(8,128)(2,1)S(1)}, bf16[768,1536]{1,0:T(8,128)(2,1)S(1)}, u32[]{:S(2)}, u32[]{:S(2)}) %collective-permute-start.31) | collective-permute-done | bytes 2359328 | tf_op jit(solution)/shard_map/ppermute | solution.py:17
  223.9 4.1 convolution_convert_fusion.5
  228.0 4.0 fusion.33
  232.7 14.7 %collective-permute-done.40 = bf16[768,768]{1,0:T(8,128)(2,1)S(1)} collective-permute-done((bf16[768,768]{1,0:T(8,128)(2,1)S(1)}, bf16[768,768]{1,0:T(8,128)(2,1)S(1)}, u32[]{:S(2)}, u32[]{:S(2)}) %collective-permute-start.40) | collective-permute-done | bytes 1179680 | tf_op jit(solution)/shard_map/ppermute | solution.py:17
  247.4 3.0 multiply_convert_fusion.3
  250.4 2.8 convolution_convert_fusion.7
  253.2 8.2 %fusion.72 = f32[16,128,2048]{2,1,0:T(8,128)} fusion(bf16[16,48,2048]{2,1,0:T(8,128)(2,1)S(1)} %bitcast.227, pred[2,16,48,128]{3,2,1,0:T(8,128)(4,1)S(1)} %compare_and_fusion), kind=kOutput, calls=%fused_computation.152 | convolution fusion | flops 402653184 | bytes 20021248 | tf_op jit(solution)/shard_map/gct,gcd->gtd/dot_general | solution.py:147
  261.4 9.1 %add_convert_fusion.1 = bf16[16,128,2048]{2,1,0:T(8,128)(2,1)S(1)} fusion(f32[16,128,2048]{2,1,0:T(8,128)} %fusion.72, bf16[16,48,2048]{2,1,0:T(8,128)(2,1)} %bitcast.240, pred[2,16,48,128]{3,2,1,0:T(8,128)(4,1)S(1)} %compare_and_fusion), kind=kOutput, calls=%fused_computation.1 | convolution fusion | flops 411041792 | bytes 28409856 | tf_op jit(solution)/shard_map/gct,gcd->gtd/dot_general | solution.py:147
  270.5 3.0 slice.177
  276.9 7.7 %fusion.20 = bf16[768,2048]{1,0:T(8,128)(2,1)S(1)} fusion(bf16[2,2048,1536]{2,1,0:T(8,128)(2,1)} %param.9, bf16[768,768]{1,0:T(8,128)(2,1)} %get-tuple-element.30, bf16[768,768]{1,0:T(8,128)(2,1)S(1)} %get-tuple-element.29), kind=kOutput, calls=%fused_computation.32 | convolution fusion | flops 4838129664 | bytes 11796480 | tf_op jit(solution)/shard_map/dot_general | solution.py:11
  284.6 4.2 fusion.32
  288.9 8.2 %fusion.71 = f32[16,128,2048]{2,1,0:T(8,128)} fusion(bf16[16,48,2048]{2,1,0:T(8,128)(2,1)S(1)} %bitcast.226, pred[2,16,48,128]{3,2,1,0:T(8,128)(4,1)S(1)} %compare_and_fusion), kind=kOutput, calls=%fused_computation.151 | convolution fusion | flops 402653184 | bytes 20021248 | tf_op jit(solution)/shard_map/gct,gcd->gtd/dot_general | solution.py:147
  297.1 6.8 %collective-permute-done.41 = bf16[768,768]{1,0:T(8,128)(2,1)S(1)} collective-permute-done((bf16[768,768]{1,0:T(8,128)(2,1)}, bf16[768,768]{1,0:T(8,128)(2,1)S(1)}, u32[]{:S(2)}, u32[]{:S(2)}) %collective-permute-start.41) | collective-permute-done | bytes 1179680 | tf_op jit(solution)/shard_map/ppermute | solution.py:17
  303.9 3.2 multiply_convert_fusion.1
  307.2 6.4 %fusion.23 = bf16[768,2048]{1,0:T(8,128)(2,1)} fusion(bf16[2,2048,1536]{2,1,0:T(8,128)(2,1)S(1)} %bitcast.246, bf16[768,768]{1,0:T(8,128)(2,1)S(1)} %get-tuple-element.28, bf16[768,768]{1,0:T(8,128)(2,1)S(1)} %get-tuple-element.27), kind=kOutput, calls=%fused_computation.33 | convolution fusion | flops 4838129664 | bytes 11796480 | tf_op jit(solution)/shard_map/dot_general | solution.py:11
  313.6 9.1 %add_convert_fusion = bf16[16,128,2048]{2,1,0:T(8,128)(2,1)S(1)} fusion(f32[16,128,2048]{2,1,0:T(8,128)} %fusion.71, bf16[16,48,2048]{2,1,0:T(8,128)(2,1)} %bitcast.241, pred[2,16,48,128]{3,2,1,0:T(8,128)(4,1)S(1)} %compare_and_fusion), kind=kOutput, calls=%fused_computation | convolution fusion | flops 411041792 | bytes 28409856 | tf_op jit(solution)/shard_map/gct,gcd->gtd/dot_general | solution.py:147
  322.7 2.5 slice.229
  325.3 3.7 copy-done.2
  330.0 3.2 pad_maximum_fusion.1
  333.2 7.7 %fusion = bf16[1,2048,1536]{2,1,0:T(8,128)(2,1)} fusion(bf16[768,2048]{1,0:T(8,128)(2,1)S(1)} %bitcast.231, bf16[768,768]{1,0:T(8,128)(2,1)S(1)} %copy-done.10, bf16[768,768]{1,0:T(8,128)(2,1)S(1)} %get-tuple-element.29), kind=kOutput, calls=%fused_computation.5 | convolution fusion | flops 4839702528 | bytes 11796480 | tf_op jit(solution)/shard_map/dot_general | solution.py:11
  341.4 8.8 %fusion.1 = bf16[1,2048,1536]{2,1,0:T(8,128)(2,1)} fusion(bf16[768,2048]{1,0:T(8,128)(2,1)} %bitcast.229, bf16[768,768]{1,0:T(8,128)(2,1)} %copy-done.15, bf16[768,768]{1,0:T(8,128)(2,1)S(1)} %copy-done.14), kind=kOutput, calls=%fused_computation.6 | convolution fusion | flops 4839702528 | bytes 11796480 | tf_op jit(solution)/shard_map/dot_general | solution.py:11
  354.4 2.7 fusion.64
  357.4 8.4 %collective-permute-done.33 = bf16[128,2048]{1,0:T(8,128)(2,1)S(1)} collective-permute-done((bf16[128,2048]{1,0:T(8,128)(2,1)S(1)}, bf16[128,2048]{1,0:T(8,128)(2,1)S(1)}, u32[]{:S(2)}, u32[]{:S(2)}) %collective-permute-start.33) | collective-permute-done | bytes 524320 | tf_op jit(solution)/shard_map/ppermute | solution.py:33
  365.8 2.2 fusion.59
  370.6 7.3 %collective-permute-done.46 = bf16[128,2048]{1,0:T(8,128)(2,1)} collective-permute-done((bf16[128,2048]{1,0:T(8,128)(2,1)}, bf16[128,2048]{1,0:T(8,128)(2,1)}, u32[]{:S(2)}, u32[]{:S(2)}) %collective-permute-start.46) | collective-permute-done | bytes 524320 | tf_op jit(solution)/shard_map/ppermute | solution.py:33
  380.7 2.5 collective-permute-done.34
  383.2 2.4 fusion.58
  387.6 6.7 %collective-permute-done.43 = bf16[128,2048]{1,0:T(8,128)(2,1)S(1)} collective-permute-done((bf16[128,2048]{1,0:T(8,128)(2,1)S(1)}, bf16[128,2048]{1,0:T(8,128)(2,1)S(1)}, u32[]{:S(2)}, u32[]{:S(2)}) %collective-permute-start.43) | collective-permute-done | bytes 524320 | tf_op jit(solution)/shard_map/ppermute | solution.py:33
  394.5 2.2 fusion.52
  398.8 7.0 %collective-permute-done.35 = bf16[128,2048]{1,0:T(8,128)(2,1)S(1)} collective-permute-done((bf16[128,2048]{1,0:T(8,128)(2,1)S(1)}, bf16[128,2048]{1,0:T(8,128)(2,1)S(1)}, u32[]{:S(2)}, u32[]{:S(2)}) %collective-permute-start.35) | collective-permute-done | bytes 524320 | tf_op jit(solution)/shard_map/ppermute | solution.py:33
  410.1 6.9 %collective-permute-done.44 = bf16[128,2048]{1,0:T(8,128)(2,1)S(1)} collective-permute-done((bf16[128,2048]{1,0:T(8,128)(2,1)S(1)}, bf16[128,2048]{1,0:T(8,128)(2,1)S(1)}, u32[]{:S(2)}, u32[]{:S(2)}) %collective-permute-start.44) | collective-permute-done | bytes 524320 | tf_op jit(solution)/shard_map/ppermute | solution.py:33
  421.5 5.2 %pad_maximum_fusion = bf16[2,2048,1536]{2,1,0:T(8,128)(2,1)} fusion(bf16[1,2048,1536]{2,1,0:T(8,128)(2,1)S(1)} %bitcast.239, bf16[1,2048,1536]{2,1,0:T(8,128)(2,1)S(1)} %bitcast.237), kind=kLoop, calls=%fused_computation.2 | loop fusion | flops 6291456 | bytes 25165824 | tf_op jit(solution)/shard_map/stack | solution.py:189
  428.7 2.3 fusion.61
  431.0 6.4 %collective-permute-done.49 = bf16[128,2048]{1,0:T(8,128)(2,1)S(1)} collective-permute-done((bf16[128,2048]{1,0:T(8,128)(2,1)S(1)}, bf16[128,2048]{1,0:T(8,128)(2,1)S(1)}, u32[]{:S(2)}, u32[]{:S(2)}) %collective-permute-start.49) | collective-permute-done | bytes 524320 | tf_op jit(solution)/shard_map/ppermute | solution.py:33
  437.4 2.3 fusion.54
  (233 shorter events, 86.4 us)
Async XLA Ops:
  7.2 432.6 %reduce-scatter.2.cloned.1.call-start = ((), (), s32[]{:S(2)}) async-start(), calls=%async_computation.1 | async-start | bytes 69632 | tf_op jit(solution)/shard_map/reduce_scatter | solution.py:198
  7.2 32.8 %collective-permute-start = (bf16[128,2048]{1,0:T(8,128)(2,1)}, bf16[128,2048]{1,0:T(8,128)(2,1)S(1)}, u32[]{:S(2)}, u32[]{:S(2)}) collective-permute-start(bf16[128,2048]{1,0:T(8,128)(2,1)} %param.6), channel_id=1, source_target_pairs={{0,4},{1,5},{4,8},{5,9},{8,12},{9,13},{12,14},{13,15},{14,10},{15,... | collective-permute-start | bytes 1572872 | tf_op jit(solution)/shard_map/ppermute | solution.py:33
  10.3 29.8 %collective-permute-start.7 = (bf16[128,2048]{1,0:T(8,128)(2,1)}, bf16[128,2048]{1,0:T(8,128)(2,1)S(1)}, u32[]{:S(2)}, u32[]{:S(2)}) collective-permute-start(bf16[128,2048]{1,0:T(8,128)(2,1)} %param.6), channel_id=1, source_target_pairs={{0,2},{1,3},{4,0},{5,1},{8,4},{9,5},{12,8},{13,9},{14,12},{15,13},... | collective-permute-start | bytes 1572872 | tf_op jit(solution)/shard_map/ppermute | solution.py:33
  10.3 74.8 %collective-permute-start.22 = (bf16[128,2048]{1,0:T(8,128)(2,1)}, bf16[128,2048]{1,0:T(8,128)(2,1)S(1)}, u32[]{:S(2)}, u32[]{:S(2)}) collective-permute-start(bf16[128,2048]{1,0:T(8,128)(2,1)} %param.6), channel_id=1, source_target_pairs={{0,1},{1,0},{2,3},{3,2},{4,5},{5,4},{6,7},{7,6},{8,9},{9,8},{10,11... | collective-permute-start | bytes 1572872 | tf_op jit(solution)/shard_map/ppermute | solution.py:38
  10.3 138.8 %collective-permute-start.14 = (bf16[128,2048]{1,0:T(8,128)(2,1)}, bf16[128,2048]{1,0:T(8,128)(2,1)S(1)}, u32[]{:S(2)}, u32[]{:S(2)}) collective-permute-start(bf16[128,2048]{1,0:T(8,128)(2,1)} %param.11), channel_id=1, source_target_pairs={{0,1},{1,0},{2,3},{3,2},{4,5},{5,4},{6,7},{7,6},{8,9},{9,8},{10,11... | collective-permute-start | bytes 1572872 | tf_op jit(solution)/shard_map/ppermute | solution.py:38
  40.0 14.3 %collective-permute-start.1 = (bf16[128,2048]{1,0:T(8,128)(2,1)S(1)}, bf16[128,2048]{1,0:T(8,128)(2,1)}, u32[]{:S(2)}, u32[]{:S(2)}) collective-permute-start(bf16[128,2048]{1,0:T(8,128)(2,1)S(1)} %collective-permute-done), channel_id=1, source_target_pairs={{0,4},{1,5},{4,8},{5,9},{8,12},{9,13},{12,14},{13,15},{14,10},{15,... | collective-permute-start | bytes 1572872 | tf_op jit(solution)/shard_map/ppermute | solution.py:33
  40.1 15.4 %collective-permute-start.8 = (bf16[128,2048]{1,0:T(8,128)(2,1)S(1)}, bf16[128,2048]{1,0:T(8,128)(2,1)}, u32[]{:S(2)}, u32[]{:S(2)}) collective-permute-start(bf16[128,2048]{1,0:T(8,128)(2,1)S(1)} %collective-permute-done.7), channel_id=1, source_target_pairs={{0,2},{1,3},{4,0},{5,1},{8,4},{9,5},{12,8},{13,9},{14,12},{15,13},... | collective-permute-start | bytes 1572872 | tf_op jit(solution)/shard_map/ppermute | solution.py:33
  54.3 13.7 %collective-permute-start.2 = (bf16[128,2048]{1,0:T(8,128)(2,1)}, bf16[128,2048]{1,0:T(8,128)(2,1)}, u32[]{:S(2)}, u32[]{:S(2)}) collective-permute-start(bf16[128,2048]{1,0:T(8,128)(2,1)} %collective-permute-done.1), channel_id=1, source_target_pairs={{0,4},{1,5},{4,8},{5,9},{8,12},{9,13},{12,14},{13,15},{14,10},{15,... | collective-permute-start | bytes 1572872 | tf_op jit(solution)/shard_map/ppermute | solution.py:33
  55.4 30.5 %collective-permute-start.23 = (bf16[128,2048]{1,0:T(8,128)(2,1)S(1)}, bf16[128,2048]{1,0:T(8,128)(2,1)S(1)}, u32[]{:S(2)}, u32[]{:S(2)}) collective-permute-start(bf16[128,2048]{1,0:T(8,128)(2,1)S(1)} %collective-permute-done), channel_id=1, source_target_pairs={{0,1},{1,0},{2,3},{3,2},{4,5},{5,4},{6,7},{7,6},{8,9},{9,8},{10,11... | collective-permute-start | bytes 1572872 | tf_op jit(solution)/shard_map/ppermute | solution.py:38
  55.5 15.1 %collective-permute-start.9 = (bf16[128,2048]{1,0:T(8,128)(2,1)}, bf16[128,2048]{1,0:T(8,128)(2,1)S(1)}, u32[]{:S(2)}, u32[]{:S(2)}) collective-permute-start(bf16[128,2048]{1,0:T(8,128)(2,1)} %collective-permute-done.8), channel_id=1, source_target_pairs={{0,2},{1,3},{4,0},{5,1},{8,4},{9,5},{12,8},{13,9},{14,12},{15,13},... | collective-permute-start | bytes 1572872 | tf_op jit(solution)/shard_map/ppermute | solution.py:33
  68.0 12.7 %collective-permute-start.3 = (bf16[128,2048]{1,0:T(8,128)(2,1)}, bf16[128,2048]{1,0:T(8,128)(2,1)S(1)}, u32[]{:S(2)}, u32[]{:S(2)}) collective-permute-start(bf16[128,2048]{1,0:T(8,128)(2,1)} %collective-permute-done.2), channel_id=1, source_target_pairs={{0,4},{1,5},{4,8},{5,9},{8,12},{9,13},{12,14},{13,15},{14,10},{15,... | collective-permute-start | bytes 1572872 | tf_op jit(solution)/shard_map/ppermute | solution.py:33
  70.5 32.6 %collective-permute-start.29 = (bf16[128,2048]{1,0:T(8,128)(2,1)S(1)}, bf16[128,2048]{1,0:T(8,128)(2,1)S(1)}, u32[]{:S(2)}, u32[]{:S(2)}) collective-permute-start(bf16[128,2048]{1,0:T(8,128)(2,1)S(1)} %collective-permute-done.7), channel_id=1, source_target_pairs={{0,1},{1,0},{2,3},{3,2},{4,5},{5,4},{6,7},{7,6},{8,9},{9,8},{10,11... | collective-permute-start | bytes 1572872 | tf_op jit(solution)/shard_map/ppermute | solution.py:38
  80.7 6.6 %collective-permute-start.24 = (bf16[128,2048]{1,0:T(8,128)(2,1)}, bf16[128,2048]{1,0:T(8,128)(2,1)S(1)}, u32[]{:S(2)}, u32[]{:S(2)}) collective-permute-start(bf16[128,2048]{1,0:T(8,128)(2,1)} %collective-permute-done.1), channel_id=1, source_target_pairs={{0,1},{1,0},{2,3},{3,2},{4,5},{5,4},{6,7},{7,6},{8,9},{9,8},{10,11... | collective-permute-start | bytes 1572872 | tf_op jit(solution)/shard_map/ppermute | solution.py:38
  85.1 14.3 %collective-permute-start.10 = (bf16[128,2048]{1,0:T(8,128)(2,1)S(1)}, bf16[128,2048]{1,0:T(8,128)(2,1)S(1)}, u32[]{:S(2)}, u32[]{:S(2)}) collective-permute-start(bf16[128,2048]{1,0:T(8,128)(2,1)S(1)} %copy-done.18), channel_id=1, source_target_pairs={{0,2},{1,3},{4,0},{5,1},{8,4},{9,5},{12,8},{13,9},{14,12},{15,13},... | collective-permute-start | bytes 1572872 | tf_op jit(solution)/shard_map/ppermute | solution.py:33
  85.9 2.3 collective-permute-start.25
  87.3 2.2 collective-permute-start.26
  88.2 12.2 %collective-permute-start.27 = (bf16[128,2048]{1,0:T(8,128)(2,1)S(1)}, bf16[128,2048]{1,0:T(8,128)(2,1)S(1)}, u32[]{:S(2)}, u32[]{:S(2)}) collective-permute-start(bf16[128,2048]{1,0:T(8,128)(2,1)S(1)} %collective-permute-done.9), channel_id=1, source_target_pairs={{0,1},{1,0},{2,3},{3,2},{4,5},{5,4},{6,7},{7,6},{8,9},{9,8},{10,11... | collective-permute-start | bytes 1572872 | tf_op jit(solution)/shard_map/ppermute | solution.py:38
  89.4 12.8 %collective-permute-start.28 = (bf16[128,2048]{1,0:T(8,128)(2,1)}, bf16[128,2048]{1,0:T(8,128)(2,1)S(1)}, u32[]{:S(2)}, u32[]{:S(2)}) collective-permute-start(bf16[128,2048]{1,0:T(8,128)(2,1)} %collective-permute-done.8), channel_id=1, source_target_pairs={{0,1},{1,0},{2,3},{3,2},{4,5},{5,4},{6,7},{7,6},{8,9},{9,8},{10,11... | collective-permute-start | bytes 1572872 | tf_op jit(solution)/shard_map/ppermute | solution.py:38
  99.4 20.0 %collective-permute-start.4 = (bf16[128,2048]{1,0:T(8,128)(2,1)S(1)}, bf16[128,2048]{1,0:T(8,128)(2,1)S(1)}, u32[]{:S(2)}, u32[]{:S(2)}) collective-permute-start(bf16[128,2048]{1,0:T(8,128)(2,1)S(1)} %copy-done.18), channel_id=1, source_target_pairs={{0,4},{1,5},{4,8},{5,9},{8,12},{9,13},{12,14},{13,15},{14,10},{15,... | collective-permute-start | bytes 1572872 | tf_op jit(solution)/shard_map/ppermute | solution.py:33
  100.4 21.3 %collective-permute-start.11 = (bf16[128,2048]{1,0:T(8,128)(2,1)S(1)}, bf16[128,2048]{1,0:T(8,128)(2,1)S(1)}, u32[]{:S(2)}, u32[]{:S(2)}) collective-permute-start(bf16[128,2048]{1,0:T(8,128)(2,1)S(1)} %collective-permute-done.10), channel_id=1, source_target_pairs={{0,2},{1,3},{4,0},{5,1},{8,4},{9,5},{12,8},{13,9},{14,12},{15,13},... | collective-permute-start | bytes 1572872 | tf_op jit(solution)/shard_map/ppermute | solution.py:33
  102.3 53.1 %collective-permute-start.21 = (bf16[128,2048]{1,0:T(8,128)(2,1)S(1)}, bf16[128,2048]{1,0:T(8,128)(2,1)S(1)}, u32[]{:S(2)}, u32[]{:S(2)}) collective-permute-start(bf16[128,2048]{1,0:T(8,128)(2,1)S(1)} %collective-permute-done.10), channel_id=1, source_target_pairs={{0,1},{1,0},{2,3},{3,2},{4,5},{5,4},{6,7},{7,6},{8,9},{9,8},{10,11... | collective-permute-start | bytes 1572872 | tf_op jit(solution)/shard_map/ppermute | solution.py:38
  117.8 114.2 %collective-permute-start.30 = (bf16[768,1536]{1,0:T(8,128)(2,1)S(1)}, bf16[768,1536]{1,0:T(8,128)(2,1)S(1)}, u32[]{:S(2)}, u32[]{:S(2)}) collective-permute-start(bf16[768,1536]{1,0:T(8,128)(2,1)S(1)} %fusion.14), channel_id=1, source_target_pairs={{0,16},{16,0},{1,17},{17,1},{2,18},{18,2},{3,19},{19,3},{4,20},{20... | collective-permute-start | bytes 7077896 | tf_op jit(solution)/shard_map/ppermute | solution.py:17
  119.4 14.1 %collective-permute-start.5 = (bf16[128,2048]{1,0:T(8,128)(2,1)S(1)}, bf16[128,2048]{1,0:T(8,128)(2,1)S(1)}, u32[]{:S(2)}, u32[]{:S(2)}) collective-permute-start(bf16[128,2048]{1,0:T(8,128)(2,1)S(1)} %collective-permute-done.4), channel_id=1, source_target_pairs={{0,4},{1,5},{4,8},{5,9},{8,12},{9,13},{12,14},{13,15},{14,10},{15,... | collective-permute-start | bytes 1572872 | tf_op jit(solution)/shard_map/ppermute | solution.py:33
  121.7 13.8 %collective-permute-start.12 = (bf16[128,2048]{1,0:T(8,128)(2,1)S(1)}, bf16[128,2048]{1,0:T(8,128)(2,1)S(1)}, u32[]{:S(2)}, u32[]{:S(2)}) collective-permute-start(bf16[128,2048]{1,0:T(8,128)(2,1)S(1)} %collective-permute-done.11), channel_id=1, source_target_pairs={{0,2},{1,3},{4,0},{5,1},{8,4},{9,5},{12,8},{13,9},{14,12},{15,13},... | collective-permute-start | bytes 1572872 | tf_op jit(solution)/shard_map/ppermute | solution.py:33
  133.5 13.2 %collective-permute-start.6 = (bf16[128,2048]{1,0:T(8,128)(2,1)S(1)}, bf16[128,2048]{1,0:T(8,128)(2,1)S(1)}, u32[]{:S(2)}, u32[]{:S(2)}) collective-permute-start(bf16[128,2048]{1,0:T(8,128)(2,1)S(1)} %collective-permute-done.5), channel_id=1, source_target_pairs={{0,4},{1,5},{4,8},{5,9},{8,12},{9,13},{12,14},{13,15},{14,10},{15,... | collective-permute-start | bytes 1572872 | tf_op jit(solution)/shard_map/ppermute | solution.py:33
  135.5 13.4 %collective-permute-start.13 = (bf16[128,2048]{1,0:T(8,128)(2,1)S(1)}, bf16[128,2048]{1,0:T(8,128)(2,1)S(1)}, u32[]{:S(2)}, u32[]{:S(2)}) collective-permute-start(bf16[128,2048]{1,0:T(8,128)(2,1)S(1)} %collective-permute-done.12), channel_id=1, source_target_pairs={{0,2},{1,3},{4,0},{5,1},{8,4},{9,5},{12,8},{13,9},{14,12},{15,13},... | collective-permute-start | bytes 1572872 | tf_op jit(solution)/shard_map/ppermute | solution.py:33
  146.7 75.8 %collective-permute-start.31 = (bf16[768,1536]{1,0:T(8,128)(2,1)S(1)}, bf16[768,1536]{1,0:T(8,128)(2,1)S(1)}, u32[]{:S(2)}, u32[]{:S(2)}) collective-permute-start(bf16[768,1536]{1,0:T(8,128)(2,1)S(1)} %fusion.17), channel_id=1, source_target_pairs={{0,16},{16,0},{1,17},{17,1},{2,18},{18,2},{3,19},{19,3},{4,20},{20... | collective-permute-start | bytes 7077896 | tf_op jit(solution)/shard_map/ppermute | solution.py:17
  149.1 2.4 collective-permute-start.16
  152.7 1.9 collective-permute-start.19
  153.4 1.9 collective-permute-start.20
  162.0 85.4 %collective-permute-start.40 = (bf16[768,768]{1,0:T(8,128)(2,1)S(1)}, bf16[768,768]{1,0:T(8,128)(2,1)S(1)}, u32[]{:S(2)}, u32[]{:S(2)}) collective-permute-start(bf16[768,768]{1,0:T(8,128)(2,1)S(1)} %fusion.45), channel_id=1, source_target_pairs={{0,16},{16,0},{1,17},{17,1},{2,18},{18,2},{3,19},{19,3},{4,20},{20... | collective-permute-start | bytes 3538952 | tf_op jit(solution)/shard_map/ppermute | solution.py:17
  275.3 74.8 %collective-permute-start.32 = (bf16[8,128,2048]{2,1,0:T(8,128)(2,1)}, bf16[8,128,2048]{2,1,0:T(8,128)(2,1)}, u32[]{:S(2)}, u32[]{:S(2)}) collective-permute-start(bf16[8,128,2048]{2,1,0:T(8,128)(2,1)} %slice.177), channel_id=1, source_target_pairs={{0,1},{1,0},{2,3},{3,2},{4,5},{5,4},{6,7},{7,6},{8,9},{9,8},{10,11... | collective-permute-start | bytes 12582920 | tf_op jit(solution)/shard_map/ppermute | solution.py:38
  275.3 28.6 %collective-permute-start.41 = (bf16[768,768]{1,0:T(8,128)(2,1)}, bf16[768,768]{1,0:T(8,128)(2,1)S(1)}, u32[]{:S(2)}, u32[]{:S(2)}) collective-permute-start(bf16[768,768]{1,0:T(8,128)(2,1)} %fusion.42), channel_id=1, source_target_pairs={{0,16},{16,0},{1,17},{17,1},{2,18},{18,2},{3,19},{19,3},{4,20},{20... | collective-permute-start | bytes 3538952 | tf_op jit(solution)/shard_map/ppermute | solution.py:17
  329.0 25.4 %collective-permute-start.42 = (bf16[8,128,2048]{2,1,0:T(8,128)(2,1)}, bf16[8,128,2048]{2,1,0:T(8,128)(2,1)}, u32[]{:S(2)}, u32[]{:S(2)}) collective-permute-start(bf16[8,128,2048]{2,1,0:T(8,128)(2,1)} %slice.229), channel_id=1, source_target_pairs={{0,1},{1,0},{2,3},{3,2},{4,5},{5,4},{6,7},{7,6},{8,9},{9,8},{10,11... | collective-permute-start | bytes 12582920 | tf_op jit(solution)/shard_map/ppermute | solution.py:38
  352.2 13.6 %collective-permute-start.33 = (bf16[128,2048]{1,0:T(8,128)(2,1)S(1)}, bf16[128,2048]{1,0:T(8,128)(2,1)S(1)}, u32[]{:S(2)}, u32[]{:S(2)}) collective-permute-start(bf16[128,2048]{1,0:T(8,128)(2,1)S(1)} %get-tuple-element.25), channel_id=1, source_target_pairs={{0,4},{1,5},{4,8},{5,9},{8,12},{9,13},{12,14},{13,15},{14,10},{15,... | collective-permute-start | bytes 1572872 | tf_op jit(solution)/shard_map/ppermute | solution.py:33
  353.3 27.4 %collective-permute-start.37 = (bf16[128,2048]{1,0:T(8,128)(2,1)S(1)}, bf16[128,2048]{1,0:T(8,128)(2,1)}, u32[]{:S(2)}, u32[]{:S(2)}) collective-permute-start(bf16[128,2048]{1,0:T(8,128)(2,1)S(1)} %get-tuple-element.26), channel_id=1, source_target_pairs={{0,2},{1,3},{4,0},{5,1},{8,4},{9,5},{12,8},{13,9},{14,12},{15,13},... | collective-permute-start | bytes 1572872 | tf_op jit(solution)/shard_map/ppermute | solution.py:33
  357.1 20.9 %collective-permute-start.46 = (bf16[128,2048]{1,0:T(8,128)(2,1)}, bf16[128,2048]{1,0:T(8,128)(2,1)}, u32[]{:S(2)}, u32[]{:S(2)}) collective-permute-start(bf16[128,2048]{1,0:T(8,128)(2,1)} %get-tuple-element.20), channel_id=1, source_target_pairs={{0,2},{1,3},{4,0},{5,1},{8,4},{9,5},{12,8},{13,9},{14,12},{15,13},... | collective-permute-start | bytes 1572872 | tf_op jit(solution)/shard_map/ppermute | solution.py:33
  368.0 15.2 %collective-permute-start.34 = (bf16[128,2048]{1,0:T(8,128)(2,1)}, bf16[128,2048]{1,0:T(8,128)(2,1)}, u32[]{:S(2)}, u32[]{:S(2)}) collective-permute-start(bf16[128,2048]{1,0:T(8,128)(2,1)} %fusion.59), channel_id=1, source_target_pairs={{0,4},{1,5},{4,8},{5,9},{8,12},{9,13},{12,14},{13,15},{14,10},{15,... | collective-permute-start | bytes 1572872 | tf_op jit(solution)/shard_map/ppermute | solution.py:33
  370.0 24.4 %collective-permute-start.43 = (bf16[128,2048]{1,0:T(8,128)(2,1)S(1)}, bf16[128,2048]{1,0:T(8,128)(2,1)S(1)}, u32[]{:S(2)}, u32[]{:S(2)}) collective-permute-start(bf16[128,2048]{1,0:T(8,128)(2,1)S(1)} %get-tuple-element.19), channel_id=1, source_target_pairs={{0,4},{1,5},{4,8},{5,9},{8,12},{9,13},{12,14},{13,15},{14,10},{15,... | collective-permute-start | bytes 1572872 | tf_op jit(solution)/shard_map/ppermute | solution.py:33
  379.6 14.9 %collective-permute-start.47 = (bf16[128,2048]{1,0:T(8,128)(2,1)S(1)}, bf16[128,2048]{1,0:T(8,128)(2,1)S(1)}, u32[]{:S(2)}, u32[]{:S(2)}) collective-permute-start(bf16[128,2048]{1,0:T(8,128)(2,1)S(1)} %fusion.50), channel_id=1, source_target_pairs={{0,2},{1,3},{4,0},{5,1},{8,4},{9,5},{12,8},{13,9},{14,12},{15,13},... | collective-permute-start | bytes 1572872 | tf_op jit(solution)/shard_map/ppermute | solution.py:33
  385.6 20.2 %collective-permute-start.35 = (bf16[128,2048]{1,0:T(8,128)(2,1)S(1)}, bf16[128,2048]{1,0:T(8,128)(2,1)S(1)}, u32[]{:S(2)}, u32[]{:S(2)}) collective-permute-start(bf16[128,2048]{1,0:T(8,128)(2,1)S(1)} %get-tuple-element.23), channel_id=1, source_target_pairs={{0,4},{1,5},{4,8},{5,9},{8,12},{9,13},{12,14},{13,15},{14,10},{15,... | collective-permute-start | bytes 1572872 | tf_op jit(solution)/shard_map/ppermute | solution.py:33
  386.6 19.4 %collective-permute-start.38 = (bf16[128,2048]{1,0:T(8,128)(2,1)S(1)}, bf16[128,2048]{1,0:T(8,128)(2,1)S(1)}, u32[]{:S(2)}, u32[]{:S(2)}) collective-permute-start(bf16[128,2048]{1,0:T(8,128)(2,1)S(1)} %get-tuple-element.24), channel_id=1, source_target_pairs={{0,2},{1,3},{4,0},{5,1},{8,4},{9,5},{12,8},{13,9},{14,12},{15,13},... | collective-permute-start | bytes 1572872 | tf_op jit(solution)/shard_map/ppermute | solution.py:33
  396.7 20.3 %collective-permute-start.44 = (bf16[128,2048]{1,0:T(8,128)(2,1)S(1)}, bf16[128,2048]{1,0:T(8,128)(2,1)S(1)}, u32[]{:S(2)}, u32[]{:S(2)}) collective-permute-start(bf16[128,2048]{1,0:T(8,128)(2,1)S(1)} %get-tuple-element.17), channel_id=1, source_target_pairs={{0,4},{1,5},{4,8},{5,9},{8,12},{9,13},{12,14},{13,15},{14,10},{15,... | collective-permute-start | bytes 1572872 | tf_op jit(solution)/shard_map/ppermute | solution.py:33
  397.5 19.8 %collective-permute-start.48 = (bf16[128,2048]{1,0:T(8,128)(2,1)S(1)}, bf16[128,2048]{1,0:T(8,128)(2,1)S(1)}, u32[]{:S(2)}, u32[]{:S(2)}) collective-permute-start(bf16[128,2048]{1,0:T(8,128)(2,1)S(1)} %get-tuple-element.18), channel_id=1, source_target_pairs={{0,2},{1,3},{4,0},{5,1},{8,4},{9,5},{12,8},{13,9},{14,12},{15,13},... | collective-permute-start | bytes 1572872 | tf_op jit(solution)/shard_map/ppermute | solution.py:33
  408.0 20.6 %collective-permute-start.39 = (bf16[128,2048]{1,0:T(8,128)(2,1)S(1)}, bf16[128,2048]{1,0:T(8,128)(2,1)S(1)}, u32[]{:S(2)}, u32[]{:S(2)}) collective-permute-start(bf16[128,2048]{1,0:T(8,128)(2,1)S(1)} %get-tuple-element.22), channel_id=1, source_target_pairs={{0,2},{1,3},{4,0},{5,1},{8,4},{9,5},{12,8},{13,9},{14,12},{15,13},... | collective-permute-start | bytes 1572872 | tf_op jit(solution)/shard_map/ppermute | solution.py:33
  409.0 19.6 %collective-permute-start.36 = (bf16[128,2048]{1,0:T(8,128)(2,1)S(1)}, bf16[128,2048]{1,0:T(8,128)(2,1)S(1)}, u32[]{:S(2)}, u32[]{:S(2)}) collective-permute-start(bf16[128,2048]{1,0:T(8,128)(2,1)S(1)} %get-tuple-element.21), channel_id=1, source_target_pairs={{0,4},{1,5},{4,8},{5,9},{8,12},{9,13},{12,14},{13,15},{14,10},{15,... | collective-permute-start | bytes 1572872 | tf_op jit(solution)/shard_map/ppermute | solution.py:33
  419.4 18.0 %collective-permute-start.49 = (bf16[128,2048]{1,0:T(8,128)(2,1)S(1)}, bf16[128,2048]{1,0:T(8,128)(2,1)S(1)}, u32[]{:S(2)}, u32[]{:S(2)}) collective-permute-start(bf16[128,2048]{1,0:T(8,128)(2,1)S(1)} %get-tuple-element.16), channel_id=1, source_target_pairs={{0,2},{1,3},{4,0},{5,1},{8,4},{9,5},{12,8},{13,9},{14,12},{15,13},... | collective-permute-start | bytes 1572872 | tf_op jit(solution)/shard_map/ppermute | solution.py:33
  420.3 17.1 %collective-permute-start.45 = (bf16[128,2048]{1,0:T(8,128)(2,1)S(1)}, bf16[128,2048]{1,0:T(8,128)(2,1)S(1)}, u32[]{:S(2)}, u32[]{:S(2)}) collective-permute-start(bf16[128,2048]{1,0:T(8,128)(2,1)S(1)} %get-tuple-element.15), channel_id=1, source_target_pairs={{0,4},{1,5},{4,8},{5,9},{8,12},{9,13},{12,14},{13,15},{14,10},{15,... | collective-permute-start | bytes 1572872 | tf_op jit(solution)/shard_map/ppermute | solution.py:33
  (40 other events, 555.7 us)
Sparse Core Ops, SparseCore 0:
  370.1 50.6 reduce-scatter.1
